TPU v7x, 256 devices: a whole 4x4x8 slice. The times are simulated.
256 devices in a mesh: lat: 4 (over y_hi, core), lon: 64 (over x, y_lo, z).
Axes of the slice: x: 4, y: 4 (y_hi: 2, y_lo: 2; y = y_hi * 2 + y_lo), z: 8, core: 2. Of those that a mesh axis runs over, the one named last changes fastest.
Arguments:
- field: bfloat16 [64, 4096, 256], P('lat', 'lon'), may hold values from -6 to 6
- filters: bfloat16 [64, 4, 9, 264], P('lat'), may hold values from -0.1875 to 0.1875
- sector_width: int32 [8], P('lat'), may hold values from 1 to 2, as said below
- block_offset: int32 [8, 4], P('lat'), may hold values from -8 to 7, as said below
- mixing: bfloat16 [9, 32, 256], replicated, may hold values from -0.375 to 0.375
Outputs:
- output: bfloat16 [64, 4096, 256], P('lat', 'lon')
Inputs may be any that keep to these rules, and one draw needn't show every extreme that they name: `sector_width`: the last row group has width 2, some row group has width 1. `block_offset`: in units of 8 longitudes; the last row group holds both ends of the range.
All inputs are finite; a program needn't handle non-finite values.
Results may differ from a plain program's by a relative error of at most 0.0049.
Values may be sent and summed in bfloat16 or wider, within the bound.
No kernel may reach another device: no remote copies, remote signals or barrier semaphores. Data moves between devices by JAX's collectives and lax.ppermute only.
A program may use at most 128 MiB of HBM per device.

v0:
```python
import jax
import jax.numpy as jnp
from jax import lax
from jax.sharding import PartitionSpec as P

K = 9
G = 8
R = 16
RG = 8
NB = 4
BW = 8
SMAX = 2


def from_behind(value, axis, steps):
    count = lax.axis_size(axis)
    pairs = [(source, (source + steps) % count) for source in range(count)]
    return lax.ppermute(value, axis, pairs)


def extended_2(value, sides, width):
    for axis, dim in sides:
        count, length = (lax.axis_size(axis), value.shape[dim])
        up = [(i, (i + 1) % count) for i in range(count - 1)]
        down = [(j, i) for i, j in up]
        last = lax.slice_in_dim(value, length - width, length, axis=dim)
        leading = lax.slice_in_dim(value, 0, width, axis=dim)
        before = lax.ppermute(last, axis, up)
        after = lax.ppermute(leading, axis, down)
        value = jnp.concatenate([before, value, after], axis=dim)
    return value


def widen(source):
    west_sectors = []
    east_sectors = []
    for distance in range(SMAX):
        west_sectors.append(from_behind(source, "lon", distance + 1))
        east_sectors.append(from_behind(source, "lon", -(distance + 1)))
    return jnp.concatenate(west_sectors[::-1] + [source] + east_sectors, axis=1)


def on_device(field, filters, sector_width, block_offset, mixing):
    rows, lon_dev, chans = field.shape
    groups = sector_width.shape[0]
    span = 2 * R + 1
    tall_rows = RG + 2 * R
    group_chans = chans // G
    flat_field = field.reshape(rows, lon_dev * chans)
    tall = extended_2(flat_field, (("lat", 0),), R)
    extended = widen(tall)
    shifts = BW * block_offset * sector_width[:, None]
    place_p = lax.broadcasted_iota(jnp.int32, (RG, span, tall_rows), 0)
    place_r = lax.broadcasted_iota(jnp.int32, (RG, span, tall_rows), 1)
    place_a = lax.broadcasted_iota(jnp.int32, (RG, span, tall_rows), 2)
    placement = (place_a == place_p + place_r).astype(jnp.float32)
    mask_rows = lax.broadcasted_iota(jnp.int32, (chans, chans), 0) // group_chans
    mask_cols = lax.broadcasted_iota(jnp.int32, (chans, chans), 1) // group_chans
    tiled_mix = jnp.tile(mixing, (1, G, 1))
    block_mix = jnp.where((mask_rows == mask_cols)[None], tiled_mix, jnp.zeros_like(tiled_mix))

    def process_group(group_index):
        start_row = group_index * RG
        group_filters = lax.dynamic_slice_in_dim(filters, start_row, RG, 0)
        response_sum = jnp.zeros((RG * K, lon_dev * chans), jnp.float32)
        for block_index in range(NB):
            start_lon = (SMAX * lon_dev + shifts[group_index, block_index]) * chans
            window = lax.dynamic_slice(
                extended, (start_row, start_lon), (tall_rows, (lon_dev + BW) * chans)
            )
            stacked = jnp.concatenate(
                [window[:, column * chans : (column + lon_dev) * chans] for column in range(BW)],
                axis=0,
            )
            weights = group_filters[:, block_index].astype(jnp.float32).reshape(RG, K, span, BW)
            padded = jnp.einsum("pkrt,pra->pkta", weights, placement)
            left_side = padded.reshape(RG * K, BW * tall_rows).astype(jnp.bfloat16)
            response_sum = response_sum + jnp.dot(
                left_side, stacked, preferred_element_type=jnp.float32
            )
        response = response_sum.astype(jnp.bfloat16).reshape(RG, K, lon_dev, chans)
        mixed = jnp.zeros((RG * lon_dev, chans), jnp.float32)
        for basis in range(K):
            mixed = mixed + jnp.dot(
                response[:, basis].reshape(RG * lon_dev, chans),
                block_mix[basis],
                preferred_element_type=jnp.float32,
            )
        return mixed.astype(jnp.bfloat16).reshape(RG, lon_dev, chans)

    results = lax.map(process_group, jnp.arange(groups, dtype=jnp.int32))
    return results.reshape(rows, lon_dev, chans)


def solution(mesh):
    return jax.shard_map(
        on_device,
        mesh=mesh,
        in_specs=(P("lat", "lon", None), P("lat", None, None, None), P("lat"), P("lat", None), P()),
        out_specs=P("lat", "lon", None),
        check_vma=False,
    )
```

profile of v0, /device:TPU:1, one launch (start us, length us, event | category | flops | bytes accessed | tf_op | source)
XLA Modules:
  0.0 320.3 jit_solution(17124768450313479132)
XLA Ops:
  1.3 6.2 %collective-permute-start = (bf16[16,16384]{1,0:T(8,128)(2,1)S(1)}, bf16[16,16384]{1,0:T(8,128)(2,1)S(1)}, u32[]{:S(2)}, u32[]{:S(2)}) collective-permute-start(bf16[16,16384]{1,0:T(8,128)(2,1)S(1)} %bitcast.204), channel_id=1, source_target_pairs={{0,64},{64,128},{128,192},{1,65},{65,129},{129,193},{2,66},{66,130... | collective-permute-start | bytes 1572872 | tf_op jit(solution)/shard_map/ppermute | solution.py:28
  15.4 5.9 %collective-permute-done.1 = bf16[16,16384]{1,0:T(8,128)(2,1)S(1)} collective-permute-done((bf16[16,16384]{1,0:T(8,128)(2,1)S(1)}, bf16[16,16384]{1,0:T(8,128)(2,1)S(1)}, u32[]{:S(2)}, u32[]{:S(2)}) %collective-permute-start.1) | collective-permute-done | bytes 524320 | tf_op jit(solution)/shard_map/ppermute | solution.py:29
  27.7 28.2 %collective-permute-start.4 = (bf16[48,16384]{1,0:T(8,128)(2,1)}, bf16[48,16384]{1,0:T(8,128)(2,1)S(1)}, u32[]{:S(2)}, u32[]{:S(2)}) collective-permute-start(bf16[48,16384]{1,0:T(8,128)(2,1)} %constant_dynamic-update-slice_fusion.1), channel_id=1, source_target_pairs={{0,63},{1,0},{2,1},{3,2},{4,3},{5,4},{6,5},{7,6},{8,7},{9,8},{10,9... | collective-permute-start | bytes 4718600 | tf_op jit(solution)/shard_map/ppermute | solution.py:18
  58.3 34.5 %collective-permute-done.2 = bf16[48,16384]{1,0:T(8,128)(2,1)} collective-permute-done((bf16[48,16384]{1,0:T(8,128)(2,1)}, bf16[48,16384]{1,0:T(8,128)(2,1)}, u32[]{:S(2)}, u32[]{:S(2)}) %collective-permute-start.2) | collective-permute-done | bytes 1572896 | tf_op jit(solution)/shard_map/ppermute | solution.py:18
  94.3 28.3 %collective-permute-done.3 = bf16[48,16384]{1,0:T(8,128)(2,1)S(1)} collective-permute-done((bf16[48,16384]{1,0:T(8,128)(2,1)}, bf16[48,16384]{1,0:T(8,128)(2,1)S(1)}, u32[]{:S(2)}, u32[]{:S(2)}) %collective-permute-start.3) | collective-permute-done | bytes 1572896 | tf_op jit(solution)/shard_map/ppermute | solution.py:18
  130.1 190.2 %while.12 = (s32[]{:T(128)}, bf16[2,8,64,256]{3,2,1,0:T(8,128)(2,1)}, s32[2]{0:T(128)S(1)}, bf16[16,4,9,264]{3,1,2,0:T(4,128)(2,1)S(1)}, s32[2,4]{1,0:T(2,128)S(...) while((s32[]{:T(128)}, ...), condition=%wide.region_1.2_spmd.clone.clone, body=%wide.region_0.1_spmd.clone.clone.sunk | while | flops 3636078592 | bytes 185017056 | solution.py:91
  143.5 5.0 %dynamic-slice_dynamic-update-slice_fusion.43 = (bf16[320,16384]{1,0:T(8,128)(2,1)}, bf16[320,16384]{1,0:T(8,128)(2,1)}, bf16[320,16384]{1,0:T(8,128)(2,1)}, bf16[320,16384]{1,0:T(8,128)(2,1)}) fusion(bf16[320,16384]{1,0:T(8,128)(2,1)} %get-tuple-element.262, bf16[48,81920]{1,0:T(8,128)(2,1)} %get-tuple-element.362, s32[]{:T(128)S(6)} %select_n.75, ...), kind=kLoop, calls=%fused_computation.10.clone.1 | loop fusion | bytes 10485780 | tf_op jit(solution)/shard_map/while
  153.4 4.9 %dynamic-slice_dynamic-update-slice_fusion.45 = (bf16[320,16384]{1,0:T(8,128)(2,1)}, bf16[320,16384]{1,0:T(8,128)(2,1)}, bf16[320,16384]{1,0:T(8,128)(2,1)}, bf16[320,16384]{1,0:T(8,128)(2,1)}) fusion(bf16[320,16384]{1,0:T(8,128)(2,1)} %get-tuple-element.270, bf16[48,81920]{1,0:T(8,128)(2,1)} %get-tuple-element.362, s32[]{:T(128)S(6)} %select_n.75, ...), kind=kLoop, calls=%fused_computation.8.clone.1 | loop fusion | bytes 10485780 | tf_op jit(solution)/shard_map/while
  163.2 4.9 %dynamic-slice_dynamic-update-slice_fusion.47 = (bf16[320,16384]{1,0:T(8,128)(2,1)}, bf16[320,16384]{1,0:T(8,128)(2,1)}, bf16[320,16384]{1,0:T(8,128)(2,1)}, bf16[320,16384]{1,0:T(8,128)(2,1)}) fusion(bf16[320,16384]{1,0:T(8,128)(2,1)} %get-tuple-element.278, bf16[48,81920]{1,0:T(8,128)(2,1)} %get-tuple-element.362, s32[]{:T(128)S(6)} %select_n.75, ...), kind=kLoop, calls=%fused_computation.6.clone.1 | loop fusion | bytes 10485780 | tf_op jit(solution)/shard_map/while
  180.0 8.5 %fusion.127 = f32[72,16384]{1,0:T(8,128)} fusion(bf16[72,320]{1,0:T(8,128)(2,1)S(1)} %convert_element_type.114, bf16[320,16384]{1,0:T(8,128)(2,1)} %get-tuple-element.289), kind=kOutput, calls=%fused_computation.107.clone.1 | convolution fusion | flops 754974720 | bytes 15250432 | tf_op jit(solution)/shard_map/while/body/eval_jaxpr/dot_general | solution.py:78
  190.1 9.9 %convolution_add_fusion.20 = f32[72,16384]{1,0:T(8,128)} fusion(f32[72,16384]{1,0:T(8,128)} %fusion.127, bf16[72,320]{1,0:T(8,128)(2,1)S(1)} %convert_element_type.115, bf16[320,16384]{1,0:T(8,128)(2,1)} %get-tuple-element.291), kind=kOutput, calls=%fused_computation.3.clone.1 | convolution fusion | flops 756154368 | bytes 19969024 | tf_op jit(solution)/shard_map/while/body/eval_jaxpr/dot_general | solution.py:78
  201.6 9.9 %convolution_add_fusion.21 = f32[72,16384]{1,0:T(8,128)} fusion(f32[72,16384]{1,0:T(8,128)} %convolution_add_fusion.20, bf16[72,320]{1,0:T(8,128)(2,1)S(1)} %convert_element_type.116, bf16[320,16384]{1,0:T(8,128)(2,1)} %get-tuple-element.293), kind=kOutput, calls=%fused_computation.2.clone.1 | convolution fusion | flops 756154368 | bytes 19969024 | tf_op jit(solution)/shard_map/while/body/eval_jaxpr/dot_general | solution.py:78
  213.0 7.8 %fusion.128 = bf16[72,16384]{1,0:T(8,128)(2,1)S(1)} fusion(f32[72,16384]{1,0:T(8,128)} %convolution_add_fusion.21, bf16[72,320]{1,0:T(8,128)(2,1)S(1)} %convert_element_type.117, bf16[320,16384]{1,0:T(8,128)(2,1)} %get-tuple-element.295), kind=kOutput, calls=%fused_computation.4.clone.1 | convolution fusion | flops 757334016 | bytes 17609728 | tf_op jit(solution)/shard_map/while/body/eval_jaxpr/dot_general | solution.py:78
  233.2 5.0 %dynamic-slice_dynamic-update-slice_fusion.42 = (bf16[320,16384]{1,0:T(8,128)(2,1)}, bf16[320,16384]{1,0:T(8,128)(2,1)}, bf16[320,16384]{1,0:T(8,128)(2,1)}, bf16[320,16384]{1,0:T(8,128)(2,1)}) fusion(bf16[320,16384]{1,0:T(8,128)(2,1)} %dynamic-slice_dynamic-update-slice_fusion.41, bf16[48,81920]{1,0:T(8,128)(2,1)} %get-tuple-element.362, ...), kind=kLoop, calls=%fused_computation.11.clone.1 | loop fusion | bytes 10485780 | tf_op jit(solution)/shard_map/while
  238.2 5.1 %dynamic-slice_dynamic-update-slice_fusion.43 = (bf16[320,16384]{1,0:T(8,128)(2,1)}, bf16[320,16384]{1,0:T(8,128)(2,1)}, bf16[320,16384]{1,0:T(8,128)(2,1)}, bf16[320,16384]{1,0:T(8,128)(2,1)}) fusion(bf16[320,16384]{1,0:T(8,128)(2,1)} %get-tuple-element.262, bf16[48,81920]{1,0:T(8,128)(2,1)} %get-tuple-element.362, s32[]{:T(128)S(6)} %select_n.75, ...), kind=kLoop, calls=%fused_computation.10.clone.1 | loop fusion | bytes 10485780 | tf_op jit(solution)/shard_map/while
  243.3 5.0 %dynamic-slice_dynamic-update-slice_fusion.44 = (bf16[320,16384]{1,0:T(8,128)(2,1)}, bf16[320,16384]{1,0:T(8,128)(2,1)}, bf16[320,16384]{1,0:T(8,128)(2,1)}, bf16[320,16384]{1,0:T(8,128)(2,1)}) fusion(bf16[320,16384]{1,0:T(8,128)(2,1)} %get-tuple-element.266, bf16[48,81920]{1,0:T(8,128)(2,1)} %get-tuple-element.362, s32[]{:T(128)S(6)} %select_n.75, ...), kind=kLoop, calls=%fused_computation.9.clone.1 | loop fusion | bytes 10485780 | tf_op jit(solution)/shard_map/while
  248.4 5.1 %dynamic-slice_dynamic-update-slice_fusion.45 = (bf16[320,16384]{1,0:T(8,128)(2,1)}, bf16[320,16384]{1,0:T(8,128)(2,1)}, bf16[320,16384]{1,0:T(8,128)(2,1)}, bf16[320,16384]{1,0:T(8,128)(2,1)}) fusion(bf16[320,16384]{1,0:T(8,128)(2,1)} %get-tuple-element.270, bf16[48,81920]{1,0:T(8,128)(2,1)} %get-tuple-element.362, s32[]{:T(128)S(6)} %select_n.75, ...), kind=kLoop, calls=%fused_computation.8.clone.1 | loop fusion | bytes 10485780 | tf_op jit(solution)/shard_map/while
  253.4 5.0 %dynamic-slice_dynamic-update-slice_fusion.46 = (bf16[320,16384]{1,0:T(8,128)(2,1)}, bf16[320,16384]{1,0:T(8,128)(2,1)}, bf16[320,16384]{1,0:T(8,128)(2,1)}, bf16[320,16384]{1,0:T(8,128)(2,1)}) fusion(bf16[320,16384]{1,0:T(8,128)(2,1)} %get-tuple-element.274, bf16[48,81920]{1,0:T(8,128)(2,1)} %get-tuple-element.362, s32[]{:T(128)S(6)} %select_n.75, ...), kind=kLoop, calls=%fused_computation.7.clone.1 | loop fusion | bytes 10485780 | tf_op jit(solution)/shard_map/while
  258.4 5.1 %dynamic-slice_dynamic-update-slice_fusion.47 = (bf16[320,16384]{1,0:T(8,128)(2,1)}, bf16[320,16384]{1,0:T(8,128)(2,1)}, bf16[320,16384]{1,0:T(8,128)(2,1)}, bf16[320,16384]{1,0:T(8,128)(2,1)}) fusion(bf16[320,16384]{1,0:T(8,128)(2,1)} %get-tuple-element.278, bf16[48,81920]{1,0:T(8,128)(2,1)} %get-tuple-element.362, s32[]{:T(128)S(6)} %select_n.75, ...), kind=kLoop, calls=%fused_computation.6.clone.1 | loop fusion | bytes 10485780 | tf_op jit(solution)/shard_map/while
  263.5 5.0 %dynamic-slice_dynamic-update-slice_fusion.48 = (bf16[320,16384]{1,0:T(8,128)(2,1)}, bf16[320,16384]{1,0:T(8,128)(2,1)}, bf16[320,16384]{1,0:T(8,128)(2,1)}, bf16[320,16384]{1,0:T(8,128)(2,1)}) fusion(bf16[320,16384]{1,0:T(8,128)(2,1)} %get-tuple-element.282, bf16[48,81920]{1,0:T(8,128)(2,1)} %get-tuple-element.362, s32[]{:T(128)S(6)} %select_n.75, ...), kind=kLoop, calls=%fused_computation.5.clone.1 | loop fusion | bytes 10485780 | tf_op jit(solution)/shard_map/while/body/eval_jaxpr/concatenate | solution.py:71
  275.7 8.5 %fusion.127 = f32[72,16384]{1,0:T(8,128)} fusion(bf16[72,320]{1,0:T(8,128)(2,1)S(1)} %convert_element_type.114, bf16[320,16384]{1,0:T(8,128)(2,1)} %get-tuple-element.289), kind=kOutput, calls=%fused_computation.107.clone.1 | convolution fusion | flops 754974720 | bytes 15250432 | tf_op jit(solution)/shard_map/while/body/eval_jaxpr/dot_general | solution.py:78
  285.8 9.9 %convolution_add_fusion.20 = f32[72,16384]{1,0:T(8,128)} fusion(f32[72,16384]{1,0:T(8,128)} %fusion.127, bf16[72,320]{1,0:T(8,128)(2,1)S(1)} %convert_element_type.115, bf16[320,16384]{1,0:T(8,128)(2,1)} %get-tuple-element.291), kind=kOutput, calls=%fused_computation.3.clone.1 | convolution fusion | flops 756154368 | bytes 19969024 | tf_op jit(solution)/shard_map/while/body/eval_jaxpr/dot_general | solution.py:78
  297.2 9.9 %convolution_add_fusion.21 = f32[72,16384]{1,0:T(8,128)} fusion(f32[72,16384]{1,0:T(8,128)} %convolution_add_fusion.20, bf16[72,320]{1,0:T(8,128)(2,1)S(1)} %convert_element_type.116, bf16[320,16384]{1,0:T(8,128)(2,1)} %get-tuple-element.293), kind=kOutput, calls=%fused_computation.2.clone.1 | convolution fusion | flops 756154368 | bytes 19969024 | tf_op jit(solution)/shard_map/while/body/eval_jaxpr/dot_general | solution.py:78
  308.6 7.8 %fusion.128 = bf16[72,16384]{1,0:T(8,128)(2,1)S(1)} fusion(f32[72,16384]{1,0:T(8,128)} %convolution_add_fusion.21, bf16[72,320]{1,0:T(8,128)(2,1)S(1)} %convert_element_type.117, bf16[320,16384]{1,0:T(8,128)(2,1)} %get-tuple-element.295), kind=kOutput, calls=%fused_computation.4.clone.1 | convolution fusion | flops 757334016 | bytes 17609728 | tf_op jit(solution)/shard_map/while/body/eval_jaxpr/dot_general | solution.py:78
  (120 shorter events, 84.7 us)
Async XLA Ops:
  1.3 12.3 %collective-permute-start = (bf16[16,16384]{1,0:T(8,128)(2,1)S(1)}, bf16[16,16384]{1,0:T(8,128)(2,1)S(1)}, u32[]{:S(2)}, u32[]{:S(2)}) collective-permute-start(bf16[16,16384]{1,0:T(8,128)(2,1)S(1)} %bitcast.204), channel_id=1, source_target_pairs={{0,64},{64,128},{128,192},{1,65},{65,129},{129,193},{2,66},{66,130... | collective-permute-start | bytes 1572872 | tf_op jit(solution)/shard_map/ppermute | solution.py:28
  7.6 13.7 %collective-permute-start.1 = (bf16[16,16384]{1,0:T(8,128)(2,1)S(1)}, bf16[16,16384]{1,0:T(8,128)(2,1)S(1)}, u32[]{:S(2)}, u32[]{:S(2)}) collective-permute-start(bf16[16,16384]{1,0:T(8,128)(2,1)S(1)} %bitcast.205), channel_id=1, source_target_pairs={{64,0},{128,64},{192,128},{65,1},{129,65},{193,129},{66,2},{130,66... | collective-permute-start | bytes 1572872 | tf_op jit(solution)/shard_map/ppermute | solution.py:29
  13.7 9.8 %copy-start.2 = (bf16[16,16384]{1,0:T(8,128)(2,1)}, bf16[16,16384]{1,0:T(8,128)(2,1)S(1)}, u32[]{:S(2)}) copy-start(bf16[16,16384]{1,0:T(8,128)(2,1)S(1)} %collective-permute-done) | copy-start | bytes 1572868
  22.1 70.7 %collective-permute-start.2 = (bf16[48,16384]{1,0:T(8,128)(2,1)}, bf16[48,16384]{1,0:T(8,128)(2,1)}, u32[]{:S(2)}, u32[]{:S(2)}) collective-permute-start(bf16[48,16384]{1,0:T(8,128)(2,1)} %constant_dynamic-update-slice_fusion.1), channel_id=1, source_target_pairs={{0,2},{1,3},{2,4},{3,5},{4,6},{5,7},{6,8},{7,9},{8,10},{9,11},{10,... | collective-permute-start | bytes 4718600 | tf_op jit(solution)/shard_map/ppermute | solution.py:18
  23.6 99.1 %copy-start.3 = (bf16[16,16384]{1,0:T(8,128)(2,1)S(1)}, bf16[16,16384]{1,0:T(8,128)(2,1)}, u32[]{:S(2)}) copy-start(bf16[16,16384]{1,0:T(8,128)(2,1)} %copy-done.2) | copy-start | bytes 1572868
  26.1 104.0 %copy-start.1 = (bf16[16,4,9,264]{3,1,2,0:T(4,128)(2,1)S(1)}, bf16[16,4,9,264]{3,1,2,0:T(4,128)(2,1)}, u32[]{:S(2)}) copy-start(bf16[16,4,9,264]{3,1,2,0:T(4,128)(2,1)} %param.8) | copy-start | bytes 912388
  26.1 96.5 %collective-permute-start.3 = (bf16[48,16384]{1,0:T(8,128)(2,1)}, bf16[48,16384]{1,0:T(8,128)(2,1)S(1)}, u32[]{:S(2)}, u32[]{:S(2)}) collective-permute-start(bf16[48,16384]{1,0:T(8,128)(2,1)} %constant_dynamic-update-slice_fusion.1), channel_id=1, source_target_pairs={{0,1},{1,2},{2,3},{3,4},{4,5},{5,6},{6,7},{7,8},{8,9},{9,10},{10,1... | collective-permute-start | bytes 4718600 | tf_op jit(solution)/shard_map/ppermute | solution.py:18
  27.7 95.1 %collective-permute-start.4 = (bf16[48,16384]{1,0:T(8,128)(2,1)}, bf16[48,16384]{1,0:T(8,128)(2,1)S(1)}, u32[]{:S(2)}, u32[]{:S(2)}) collective-permute-start(bf16[48,16384]{1,0:T(8,128)(2,1)} %constant_dynamic-update-slice_fusion.1), channel_id=1, source_target_pairs={{0,63},{1,0},{2,1},{3,2},{4,3},{5,4},{6,5},{7,6},{8,7},{9,8},{10,9... | collective-permute-start | bytes 4718600 | tf_op jit(solution)/shard_map/ppermute | solution.py:18
  56.0 70.9 %collective-permute-start.5 = (bf16[48,16384]{1,0:T(8,128)(2,1)}, bf16[48,16384]{1,0:T(8,128)(2,1)S(1)}, u32[]{:S(2)}, u32[]{:S(2)}) collective-permute-start(bf16[48,16384]{1,0:T(8,128)(2,1)} %constant_dynamic-update-slice_fusion.1), channel_id=1, source_target_pairs={{0,62},{1,63},{2,0},{3,1},{4,2},{5,3},{6,4},{7,5},{8,6},{9,7},{10,... | collective-permute-start | bytes 4718600 | tf_op jit(solution)/shard_map/ppermute | solution.py:18
  127.0 3.1 copy-start
  221.4 2.4 copy-start.4
  223.8 0.8 copy-start.5
  317.0 2.4 copy-start.4
  319.5 0.8 copy-start.5
where the time goes:
time: 321 us; the launch traced here: 320 us
  local copies, waits for them, and re-layouts  111 us (35%)
  matrix products  77.9 us (24%)
  waiting for transfers between devices  76.7 us (24%)
  starting transfers between devices  41.7 us (13%)
  loops' own time  10.1 us (3%)
    dot_general x8, matrix products, process_group(): jnp.dot(left_side, stacked, preferred_element_type=jnp.float32)  72.2 us
    while x24, local copies, waits for them, and re-layouts  67.6 us
    ppermute x4, waiting for transfers between devices, from_behind(): return lax.ppermute(value, axis, pairs)  66.7 us
    ppermute x4, starting transfers between devices, from_behind(): return lax.ppermute(value, axis, pairs)  33.5 us
    concatenate x4, local copies, waits for them, and re-layouts, process_group(): jnp.concatenate([window[:, column * chans:(column + lon_dev) * chans] for...  18.3 us
    another operation x1, loops' own time, on_device(): results = lax.map(process_group, jnp.arange(groups, dtype=jnp.int32))  10.1 us
    reshape x16, local copies, waits for them, and re-layouts, process_group(): group_filters[:, block_index].astype(jnp.float32).reshape(RG, K, span, BW)  9 us
    unnamed x17, local copies, waits for them, and re-layouts  7.92 us
  transfers between devices with their start and end apart: 6, of which 5 were waited for; matrix products, arithmetic and copies ran while one was open for 2% of the time, Pallas kernels for 0%

commit v1 on v0

v1 whole, which is shorter than its diff:
```python
import functools

import jax
import jax.numpy as jnp
from jax import lax
from jax.experimental import pallas as pl
from jax.experimental.pallas import tpu as pltpu
from jax.sharding import PartitionSpec as P

K = 9
G = 8
R = 16
RG = 8
NB = 4
BW = 8
SMAX = 2
SPAN = 2 * R + 1
J = 2
T = BW + J - 1

SWAP = [(0, 1), (1, 0), (2, 3), (3, 2)]
ACROSS = [(0, 2), (2, 0), (1, 3), (3, 1)]


def from_behind(value, steps):
    count = lax.axis_size("lon")
    pairs = [(source, (source + steps) % count) for source in range(count)]
    return lax.ppermute(value, "lon", pairs)


def conv_kernel(depths, shift_ref, *refs):
    parts = len(depths)
    pieces = [refs[5 * i : 5 * i + 5] for i in range(parts)]
    refs = refs[5 * parts :]
    lhs_ref, mix_ref, out_ref = refs[:3]
    exts = refs[3 : 3 + parts]
    resp_ref, mixed_ref, sems = refs[3 + parts :]
    lon = pieces[0][0].shape[0]
    half = lon // 2
    steps = half // J
    copies = []
    for i in range(parts):
        for n in range(5):
            copy = pltpu.make_async_copy(
                pieces[i][n], exts[i].at[pl.ds(n * lon, lon)], sems.at[i, n]
            )
            copy.start()
            copies.append(copy)
    for copy in copies:
        copy.wait()

    def group(g, carry):
        def step(jb, carry):
            columns = []
            for side in range(2):
                rows = []
                for i in range(parts):
                    for b in range(NB):
                        start = SMAX * lon + shift_ref[g, b] + jb * J + side * half
                        window = exts[i][pl.ds(start, T)]
                        rows.append(window.reshape(T * depths[i], window.shape[2]))
                columns.append(jnp.concatenate(rows, axis=0))
            right = jnp.concatenate(columns, axis=1)
            resp = jnp.dot(lhs_ref[g], right, preferred_element_type=jnp.float32)
            resp = resp.astype(jnp.bfloat16)
            width = resp.shape[1]
            for k in range(K):
                resp_ref[pl.ds(pl.multiple_of(jb * 16, 16), 16), k * width : (k + 1) * width] = (
                    resp[k * 16 : (k + 1) * 16]
                )
            return carry

        lax.fori_loop(0, steps, step, 0, unroll=2)
        mixed = jnp.dot(resp_ref[...], mix_ref[...], preferred_element_type=jnp.float32)
        chans = mixed.shape[1] // 2
        for side in range(2):
            mixed_ref[side] = mixed[:, side * chans : (side + 1) * chans]
            for p in range(RG):
                rows = mixed_ref[side, pl.ds(p, half, stride=RG), :]
                out_ref[g, p, side * half : (side + 1) * half, :] = rows.astype(jnp.bfloat16)
        return carry

    lax.fori_loop(0, 2, group, 0)


def conv(shifts, pieces, lhs, mix):
    parts = len(pieces)
    lon, _, chans = pieces[0][0].shape
    depths = [p[0].shape[1] for p in pieces]
    vmem = pl.BlockSpec(memory_space=pltpu.VMEM)
    hbm = pl.BlockSpec(memory_space=pl.ANY)
    flat = [x for p in pieces for x in p]
    out = pl.pallas_call(
        functools.partial(conv_kernel, depths),
        out_shape=jax.ShapeDtypeStruct((2, RG, lon, chans), jnp.bfloat16),
        in_specs=[pl.BlockSpec(memory_space=pltpu.SMEM)] + [hbm] * len(flat) + [vmem, vmem],
        out_specs=vmem,
        scratch_shapes=[pltpu.VMEM((5 * lon, d, chans), jnp.bfloat16) for d in depths]
        + [
            pltpu.VMEM((lon // 2 * RG, K * 2 * chans), jnp.bfloat16),
            pltpu.VMEM((2, lon // 2 * RG, chans), jnp.float32),
            pltpu.SemaphoreType.DMA((parts, 5)),
        ],
        compiler_params=pltpu.CompilerParams(vmem_limit_bytes=48 << 20),
        cost_estimate=pl.CostEstimate(
            flops=2 * lhs.size * lon // J * chans, bytes_accessed=8 << 20, transcendentals=0
        ),
    )(shifts, *flat, lhs, mix)
    return out.reshape(2 * RG, lon, chans)


def left_sides(weights):
    rows = weights.shape[0]
    tall = rows + 2 * R
    at = lambda d: lax.broadcasted_iota(jnp.int32, (rows, SPAN, BW, J, T, tall), d)
    place = ((at(5) == at(0) + at(1)) & (at(4) == at(2) + at(3))).astype(jnp.bfloat16)
    place = place.reshape(rows, SPAN * BW, J * T * tall)
    flat = weights.reshape(rows, NB * K, SPAN * BW)
    spread = jnp.einsum("ixr,irc->ixc", flat, place, preferred_element_type=jnp.float32)
    spread = spread.astype(jnp.bfloat16).reshape(2, RG, NB, K, J, T, tall)
    return spread.transpose(0, 3, 4, 1, 2, 5, 6).reshape(2, K * J * RG, NB, T, tall)


def on_device(field, filters, sector_width, block_offset, mixing):
    rows, lon, chans = field.shape
    half = chans // 2
    lat = lax.axis_index("lat")
    upper, core = lat // 2, lat % 2

    turned = field.transpose(1, 0, 2)
    low, high = turned[:, :, :half], turned[:, :, half:]
    first = core == 0
    mine = jnp.where(first, low, high)
    got = lax.ppermute(jnp.where(first, high, low), "lat", SWAP)
    top, bottom = jnp.where(first, mine, got), jnp.where(first, got, mine)
    own = jnp.concatenate([top, bottom], axis=1)
    edge = lax.ppermute(jnp.where(upper == 0, bottom, top), "lat", ACROSS)

    def sectors(x):
        west, east = from_behind(x, 1), from_behind(x, -1)
        return [from_behind(west, 1), west, x, east, from_behind(east, -1)]

    own_sectors = sectors(own)
    edge_sectors = sectors(edge)

    shifts = BW * block_offset * sector_width[:, None]
    other_shifts = lax.ppermute(shifts, "lat", SWAP)
    other_filters = lax.ppermute(filters, "lat", SWAP)
    far = core == upper
    far_shifts = jnp.where(far, shifts, other_shifts)
    near_shifts = jnp.where(far, other_shifts, shifts)
    far_left = left_sides(jnp.where(far, filters, other_filters))
    near_left = left_sides(jnp.where(far, other_filters, filters))

    def columns(left, start, width):
        left = lax.dynamic_slice_in_dim(left, start, width, axis=4)
        return left.reshape(2, K * J * RG, NB * T * width)

    far_lhs = columns(far_left, R * (1 - upper), 2 * R)
    near_lhs = jnp.concatenate(
        [columns(near_left, R * upper, 2 * R), columns(near_left, 2 * R * (1 - upper), R)], axis=2
    )

    group_chans = chans // G
    side = lax.dynamic_slice_in_dim(mixing, core * half, half, axis=2)
    tiled = jnp.tile(side, (1, chans // group_chans, 2))
    row_at = lax.broadcasted_iota(jnp.int32, (chans, chans), 0) // group_chans
    col_at = lax.broadcasted_iota(jnp.int32, (chans, chans), 1) // group_chans
    mix = jnp.where((row_at == col_at)[None], tiled, jnp.zeros_like(tiled))
    mix = mix.reshape(K * chans, chans)

    far_out = conv(far_shifts, [own_sectors], far_lhs, mix)
    near_out = conv(near_shifts, [own_sectors, edge_sectors], near_lhs, mix)

    kept = jnp.where(far, far_out, near_out)
    other = lax.ppermute(jnp.where(far, near_out, far_out), "lat", SWAP)
    return jnp.concatenate([jnp.where(first, kept, other), jnp.where(first, other, kept)], axis=2)


def solution(mesh):
    return jax.shard_map(
        on_device,
        mesh=mesh,
        in_specs=(P("lat", "lon", None), P("lat", None, None, None), P("lat"), P("lat", None), P()),
        out_specs=P("lat", "lon", None),
        check_vma=False,
    )
```

time: 321 us -> 109 us (0.34)
  waiting for transfers between devices: 76.7 us -> 1.19 us
  matrix products: 77.9 us -> 7.64 us
  local copies, waits for them, and re-layouts: 111 us -> 50.1 us
  Pallas kernels: 0 us -> 20.5 us
  starting transfers between devices: 41.7 us -> 24.7 us
  loops' own time: 10.1 us -> 0 us
    ppermute x6 -> x13, waiting for transfers between devices: 76.7 us -> 1.19 us  [the longest x1 1.16 us: on_device(): other = lax.ppermute(jnp.where(far, near_out, far_out), 'lat', SWAP)]
    dot_general x34 -> x2, matrix products: 77.9 us -> 7.64 us  [left_sides(): jnp.einsum('ixr,irc->ixc', flat, place, preferred_element_type=jnp.float32)]
    while x24 -> x0, local copies, waits for them, and re-layouts: 67.6 us -> none
    pallas_call x0 -> x2, Pallas kernels: none -> 20.5 us  [conv(): pl.pallas_call(functools.partial(conv_kernel, depths), out_shape=jax.Shap...]
    concatenate x6 -> x0, local copies, waits for them, and re-layouts: 19.2 us -> none  [the longest x4 18.3 us: process_group(): jnp.concatenate([window[:, column * chans:(column + lon_dev) * chans] for...]
    ppermute x6 -> x13, starting transfers between devices: 41.7 us -> 24.7 us  [the longest x8 15.9 us: from_behind(): return lax.ppermute(value, 'lon', pairs)]
    dynamic_slice x4 -> x7, local copies, waits for them, and re-layouts: 2.52 us -> 18.4 us  [the longest x6 18.4 us: columns(): left = lax.dynamic_slice_in_dim(left, start, width, axis=4)]
    another operation x1 -> x0, loops' own time: 10.1 us -> none  [on_device(): results = lax.map(process_group, jnp.arange(groups, dtype=jnp.int32))]
  transfers between devices with their start and end apart: 6 -> 13, of which waited for: 5 -> 1; matrix products, arithmetic and copies ran while one was open for 2% -> 54% of each run, Pallas kernels for 0% -> 8%
where the time goes in v1:
time: 109 us; the launch traced here: 108 us
  local copies, waits for them, and re-layouts  50.1 us (46%)
  starting transfers between devices  24.7 us (23%)
  Pallas kernels  20.5 us (19%)
  matrix products  7.64 us (7%)
  other arithmetic  3.74 us (3%)
  waiting for transfers between devices  1.19 us (1%)
    pallas_call x2, Pallas kernels, conv(): pl.pallas_call(functools.partial(conv_kernel, depths), out_shape=jax.Shap...  20.5 us
    dynamic_slice x6, local copies, waits for them, and re-layouts, columns(): left = lax.dynamic_slice_in_dim(left, start, width, axis=4)  18.4 us
    ppermute x8, starting transfers between devices, from_behind(): return lax.ppermute(value, 'lon', pairs)  15.9 us
    reshape x2, local copies, waits for them, and re-layouts, left_sides(): spread = spread.astype(jnp.bfloat16).reshape(2, RG, NB, K, J, T, tall)  11.6 us
    dot_general x2, matrix products, left_sides(): jnp.einsum('ixr,irc->ixc', flat, place, preferred_element_type=jnp.float32)  7.64 us
    transpose x2, local copies, waits for them, and re-layouts, left_sides(): spread.transpose(0, 3, 4, 1, 2, 5, 6).reshape(2, K * J * RG, NB, T, tall)  6.95 us
    reshape x3, local copies, waits for them, and re-layouts, columns(): return left.reshape(2, K * J * RG, NB * T * width)  4 us
    iota x10, local copies, waits for them, and re-layouts, left_sides(): lax.broadcasted_iota(jnp.int32, (rows, SPAN, BW, J, T, tall), d)  3.33 us
  transfers between devices with their start and end apart: 13, of which 1 were waited for; matrix products, arithmetic and copies ran while one was open for 54% of the time, Pallas kernels for 8%

profile of v1, /device:TPU:1, one launch (start us, length us, event | category | flops | bytes accessed | tf_op | source)
XLA Modules:
  0.0 108.4 jit_solution(17404732479198164402)
XLA Ops:
  0.0 1.9 %copy.22 = bf16[16,4,9,264]{3,0,2,1:T(8,128)(2,1)} copy(bf16[16,4,9,264]{3,1,2,0:T(4,128)(2,1)} %param.6) | data formatting | bytes 608256 | tf_op args[1]
  1.9 3.2 %collective-permute-start.6 = (bf16[16,4,9,264]{3,0,2,1:T(8,128)(2,1)}, bf16[16,4,9,264]{3,0,2,1:T(8,128)(2,1)}, u32[]{:S(2)}, u32[]{:S(2)}) collective-permute-start(bf16[16,4,9,264]{3,0,2,1:T(8,128)(2,1)} %copy.22), channel_id=1, source_target_pairs={{0,64},{64,0},{128,192},{192,128},{1,65},{65,1},{129,193},{193,129... | collective-permute-start | bytes 912392 | tf_op jit(solution)/shard_map/ppermute | solution.py:148
  5.1 1.3 %copy.45 = bf16[16,64,256]{2,0,1:T(8,128)(2,1)S(1)} copy(bf16[16,64,256]{2,1,0:T(8,128)(2,1)} %param.5) | data formatting | bytes 1048576 | tf_op args[0]
  13.4 7.1 %collective-permute-start.4 = (bf16[64,32,128]{2,1,0:T(8,128)(2,1)S(1)}, bf16[64,32,128]{2,1,0:T(8,128)(2,1)}, u32[]{:S(2)}, u32[]{:S(2)}) collective-permute-start(bf16[64,32,128]{2,1,0:T(8,128)(2,1)S(1)} %pad_maximum_fusion.1.refs_2_), channel_id=1, source_target_pairs={{0,63},{1,0},{2,1},{3,2},{4,3},{5,4},{6,5},{7,6},{8,7},{9,8},{10,9... | collective-permute-start | bytes 1572872 | tf_op jit(solution)/shard_map/ppermute | solution.py:28
  20.5 2.6 %collective-permute-start.7 = (bf16[64,16,128]{2,1,0:T(8,128)(2,1)}, bf16[64,16,128]{2,1,0:T(8,128)(2,1)S(1)}, u32[]{:S(2)}, u32[]{:S(2)}) collective-permute-start(bf16[64,16,128]{2,1,0:T(8,128)(2,1)} %get-tuple-element.5), channel_id=1, source_target_pairs={{0,128},{128,0},{64,192},{192,64},{1,129},{129,1},{65,193},{193,65... | collective-permute-start | bytes 786440 | tf_op jit(solution)/shard_map/ppermute | solution.py:137
  24.3 3.3 %convolution_convert_fusion = bf16[16,36,864]{2,1,0:T(8,128)(2,1)S(1)} fusion(s32[864]{0:T(1024)S(1)} %copy-done.8, s32[264]{0:T(512)S(1)} %copy-done.11, s32[864]{0:T(1024)S(1)} %copy-done.7, s32[264]{0:T(512)S(1)} %copy-done.10, s32[864]{0:T(1024)S(1)} %copy-done.6, bf16[16,36,264]{2,0,1:T(8,128)(2,1)S(1)} %bitcast.38), kind=kOutput, calls=%fused_computation.4 | convolution fusion | flops 281511936 | bytes 1311936 | tf_op jit(solution)/shard_map/ixr,irc->ixc/dot_general | solution.py:119
  27.7 4.3 %convolution_convert_fusion.1 = bf16[16,36,864]{2,1,0:T(8,128)(2,1)} fusion(s32[864]{0:T(1024)S(1)} %copy-done.8, s32[264]{0:T(512)S(1)} %copy-done.11, s32[864]{0:T(1024)S(1)} %copy-done.7, s32[264]{0:T(512)S(1)} %copy-done.10, s32[864]{0:T(1024)S(1)} %copy-done.6, bf16[16,36,264]{2,0,1:T(8,128)(2,1)S(1)} %bitcast.37), kind=kOutput, calls=%fused_computation.5 | convolution fusion | flops 281511936 | bytes 1311936 | tf_op jit(solution)/shard_map/ixr,irc->ixc/dot_general | solution.py:119
  32.1 5.8 %reshape.132 = bf16[2,8,4,9,2,9,48]{6,5,4,1,0,3,2:T(8,128)(2,1)} reshape(bf16[16,36,864]{2,0,1:T(8,128)(2,1)S(1)} %copy.30) | data formatting | bytes 1990656 | tf_op jit(solution)/shard_map/reshape | solution.py:120
  37.9 3.4 %copy.31 = bf16[2,9,2,8,4,9,48]{6,3,2,1,5,4,0:T(8,128)(2,1)S(1)} copy(bf16[2,9,2,8,4,9,48]{6,5,2,3,0,1,4:T(8,128)(2,1)} %bitcast.28) | data formatting | bytes 1990656 | tf_op jit(solution)/shard_map/transpose | solution.py:121
  41.3 2.3 %constant_dynamic-slice_fusion.1 = bf16[2,144,4,9,32]{4,1,3,2,0:T(8,128)(2,1)} fusion(bf16[2,144,4,9,48]{4,1,3,2,0:T(8,128)(2,1)S(1)} %bitcast.26, s32[]{:T(128)S(6)} %select_n.144), kind=kLoop, calls=%fused_computation.29 | loop fusion | bytes 1327108 | tf_op jit(solution)/shard_map/dynamic_slice | solution.py:156
  45.1 5.7 %collective-permute-start.5 = (bf16[64,32,128]{2,1,0:T(8,128)(2,1)}, bf16[64,32,128]{2,1,0:T(8,128)(2,1)}, u32[]{:S(2)}, u32[]{:S(2)}) collective-permute-start(bf16[64,32,128]{2,1,0:T(8,128)(2,1)} %collective-permute-done.4.refs_3_), channel_id=1, source_target_pairs={{0,63},{1,0},{2,1},{3,2},{4,3},{5,4},{6,5},{7,6},{8,7},{9,8},{10,9... | collective-permute-start | bytes 1572872 | tf_op jit(solution)/shard_map/ppermute | solution.py:28
  50.8 2.4 %constant_dynamic-slice_fusion = bf16[2,144,4,9,16]{4,1,3,2,0:T(8,128)(2,1)} fusion(bf16[2,144,4,9,48]{4,1,3,2,0:T(8,128)(2,1)S(1)} %bitcast.27, s32[]{:T(128)S(6)} %select_n.145), kind=kLoop, calls=%fused_computation.28 | loop fusion | bytes 663556 | tf_op jit(solution)/shard_map/dynamic_slice | solution.py:156
  53.1 4.1 %copy.32 = bf16[2,144,4,9,32]{1,4,3,2,0:T(8,128)(2,1)} copy(bf16[2,144,4,9,32]{4,1,3,2,0:T(8,128)(2,1)} %constant_dynamic-slice_fusion.1) | data formatting | bytes 1327104 | tf_op jit(solution)/shard_map/dynamic_slice | solution.py:156
  57.2 2.2 %copy.34 = bf16[2,144,1152]{2,1,0:T(8,128)(2,1)} copy(bf16[2,144,1152]{1,2,0:T(8,128)(2,1)} %bitcast.32) | data formatting | bytes 1327104 | tf_op jit(solution)/shard_map/reshape | solution.py:157
  59.5 3.2 %copy.33 = bf16[2,144,4,9,16]{1,4,3,2,0:T(8,128)(2,1)S(1)} copy(bf16[2,144,4,9,16]{4,1,3,2,0:T(8,128)(2,1)} %constant_dynamic-slice_fusion) | data formatting | bytes 663552 | tf_op jit(solution)/shard_map/dynamic_slice | solution.py:156
  62.9 1.4 %copy.24 = bf16[16,36,864]{2,0,1:T(8,128)(2,1)S(1)} copy(bf16[16,36,864]{2,1,0:T(8,128)(2,1)} %convolution_convert_fusion.1) | data formatting | bytes 1990656 | tf_op jit(solution)/shard_map/convert_element_type | solution.py:120
  64.3 5.8 %reshape.128 = bf16[2,8,4,9,2,9,48]{6,5,4,1,0,3,2:T(8,128)(2,1)} reshape(bf16[16,36,864]{2,0,1:T(8,128)(2,1)S(1)} %copy.24) | data formatting | bytes 1990656 | tf_op jit(solution)/shard_map/reshape | solution.py:120
  70.1 3.5 %copy.25 = bf16[2,9,2,8,4,9,48]{6,3,2,1,5,4,0:T(8,128)(2,1)S(1)} copy(bf16[2,9,2,8,4,9,48]{6,5,2,3,0,1,4:T(8,128)(2,1)} %bitcast.29) | data formatting | bytes 1990656 | tf_op jit(solution)/shard_map/transpose | solution.py:121
  75.3 2.3 %constant_dynamic-slice_fusion.3 = bf16[2,144,4,9,32]{4,1,3,2,0:T(8,128)(2,1)} fusion(bf16[2,144,4,9,48]{4,1,3,2,0:T(8,128)(2,1)S(1)} %bitcast.30, s32[]{:T(128)S(6)} %select_n.135), kind=kLoop, calls=%fused_computation.31 | loop fusion | bytes 1327108 | tf_op jit(solution)/shard_map/dynamic_slice | solution.py:156
  77.6 4.1 %copy.26 = bf16[2,144,4,9,32]{1,4,3,2,0:T(8,128)(2,1)} copy(bf16[2,144,4,9,32]{4,1,3,2,0:T(8,128)(2,1)} %constant_dynamic-slice_fusion.3) | data formatting | bytes 1327104 | tf_op jit(solution)/shard_map/dynamic_slice | solution.py:156
  81.7 1.5 %copy.27.refs_5_ = bf16[2,144,1152]{2,1,0:T(8,128)(2,1)S(1)} copy(bf16[2,144,1152]{1,2,0:T(8,128)(2,1)} %bitcast.33) | data formatting | bytes 1327104 | tf_op jit(solution)/shard_map/reshape | solution.py:157
  83.3 9.1 %shard_map.55 = bf16[2,8,64,128]{3,2,1,0:T(8,128)(2,1)S(1)} custom-call(s32[2,4]{1,0:T(2,128)S(1)} %get-tuple-element.14.shift_ref, bf16[64,32,128]{2,1,0:T(8,128)(2,1)} %collective-permute-done.3.refs_0_, bf16[64,32,128]{2,1,0:T(8,128)(2,1)} %collective-permute-done.2.refs_1_, bf16[64,32,128]{2,1,0:T(8,128)(2,1)S(1)} %pad_maximum_fusion.1.refs_2_, ...), custom_call_target="tpu_custom_call" | custom-call | flops 2717908992 | bytes 8388608 | tf_op jit(solution)/shard_map/pallas_call | solution.py:93
  92.4 11.5 %shard_map.56 = bf16[2,8,64,128]{3,2,1,0:T(8,128)(2,1)S(1)} custom-call(s32[2,4]{1,0:T(2,128)S(1)} %get-tuple-element.15.shift_ref, bf16[64,32,128]{2,1,0:T(8,128)(2,1)} %collective-permute-done.3.refs_0_, bf16[64,32,128]{2,1,0:T(8,128)(2,1)} %collective-permute-done.2.refs_1_, bf16[64,32,128]{2,1,0:T(8,128)(2,1)S(1)} %pad_maximum_fusion.1.refs_2_, ...), custom_call_target="tpu_custom_call" | custom-call | flops 4076863488 | bytes 8388608 | tf_op jit(solution)/shard_map/pallas_call | solution.py:93
  103.9 2.4 %collective-permute-start.12 = (bf16[16,64,128]{2,1,0:T(8,128)(2,1)S(1)}, bf16[16,64,128]{2,1,0:T(8,128)(2,1)S(1)}, u32[]{:S(2)}, u32[]{:S(2)}) collective-permute-start(bf16[16,64,128]{2,1,0:T(8,128)(2,1)S(1)} %bitcast.39), channel_id=1, source_target_pairs={{0,64},{64,0},{128,192},{192,128},{1,65},{65,1},{129,193},{193,129... | collective-permute-start | bytes 786440 | tf_op jit(solution)/shard_map/ppermute | solution.py:176
  (76 shorter events, 13.5 us)
Async XLA Ops:
  0.0 7.4 %copy-start = (bf16[9,32,256]{2,1,0:T(8,128)(2,1)S(1)}, bf16[9,32,256]{2,1,0:T(8,128)(2,1)}, u32[]{:S(2)}) copy-start(bf16[9,32,256]{2,1,0:T(8,128)(2,1)} %param.9) | copy-start | bytes 442372
  0.0 6.6 %copy-start.9 = (s32[2,4]{1,0:T(2,128)S(1)}, s32[2,4]{1,0:T(2,128)}, u32[]{:S(2)}) copy-start(s32[2,4]{1,0:T(2,128)} %param.8) | copy-start | bytes 100
  1.9 21.3 %collective-permute-start.6 = (bf16[16,4,9,264]{3,0,2,1:T(8,128)(2,1)}, bf16[16,4,9,264]{3,0,2,1:T(8,128)(2,1)}, u32[]{:S(2)}, u32[]{:S(2)}) collective-permute-start(bf16[16,4,9,264]{3,0,2,1:T(8,128)(2,1)} %copy.22), channel_id=1, source_target_pairs={{0,64},{64,0},{128,192},{192,128},{1,65},{65,1},{129,193},{193,129... | collective-permute-start | bytes 912392 | tf_op jit(solution)/shard_map/ppermute | solution.py:148
  6.5 5.8 %collective-permute-start.1 = (bf16[64,16,128]{2,1,0:T(8,128)(2,1)S(1)}, bf16[64,16,128]{2,1,0:T(8,128)(2,1)S(1)}, u32[]{:S(2)}, u32[]{:S(2)}) collective-permute-start(bf16[64,16,128]{2,1,0:T(8,128)(2,1)S(1)} %broadcast_select_fusion.5), channel_id=1, source_target_pairs={{0,64},{64,0},{128,192},{192,128},{1,65},{65,1},{129,193},{193,129... | collective-permute-start | bytes 786440 | tf_op jit(solution)/shard_map/ppermute | solution.py:134
  6.7 5.5 %collective-permute-start = (s32[2,4]{1,0:T(2,128)S(1)}, s32[2,4]{1,0:T(2,128)S(1)}, u32[]{:S(2)}, u32[]{:S(2)}) collective-permute-start(s32[2,4]{1,0:T(2,128)S(1)} %broadcast_multiply_fusion), channel_id=1, source_target_pairs={{0,64},{64,0},{128,192},{192,128},{1,65},{65,1},{129,193},{193,129... | collective-permute-start | bytes 104 | tf_op jit(solution)/shard_map/ppermute | solution.py:147
  11.9 11.2 %copy-start.5 = (bf16[16,4,9,264]{3,1,2,0:T(4,128)(2,1)S(1)}, bf16[16,4,9,264]{3,1,2,0:T(4,128)(2,1)}, u32[]{:S(2)}) copy-start(bf16[16,4,9,264]{3,1,2,0:T(4,128)(2,1)} %param.6) | copy-start | bytes 912388
  12.1 71.1 %copy-start.1 = (bf16[2304,256]{1,0:T(8,128)(2,1)}, bf16[2304,256]{1,0:T(8,128)(2,1)S(1)}, u32[]{:S(2)}) copy-start(bf16[2304,256]{1,0:T(8,128)(2,1)S(1)} %bitcast_select_fusion.refs_6_.refs_11_) | copy-start | bytes 3538948
  12.1 12.1 %copy-start.6 = (s32[864]{0:T(1024)S(1)}, s32[864]{0:T(1024)}, u32[]{:S(2)}) copy-start(s32[864]{0:T(1024)} %iota.124) | copy-start | bytes 10372
  12.2 12.1 %copy-start.7 = (s32[864]{0:T(1024)S(1)}, s32[864]{0:T(1024)}, u32[]{:S(2)}) copy-start(s32[864]{0:T(1024)} %iota.131) | copy-start | bytes 10372
  12.2 12.1 %copy-start.8 = (s32[864]{0:T(1024)S(1)}, s32[864]{0:T(1024)}, u32[]{:S(2)}) copy-start(s32[864]{0:T(1024)} %iota.137) | copy-start | bytes 10372
  12.2 12.1 %copy-start.10 = (s32[264]{0:T(512)S(1)}, s32[264]{0:T(512)}, u32[]{:S(2)}) copy-start(s32[264]{0:T(512)} %iota.128) | copy-start | bytes 3172
  12.2 12.1 %copy-start.11 = (s32[264]{0:T(512)S(1)}, s32[264]{0:T(512)}, u32[]{:S(2)}) copy-start(s32[264]{0:T(512)} %iota.134) | copy-start | bytes 3172
  13.3 31.8 %collective-permute-start.2 = (bf16[64,32,128]{2,1,0:T(8,128)(2,1)S(1)}, bf16[64,32,128]{2,1,0:T(8,128)(2,1)}, u32[]{:S(2)}, u32[]{:S(2)}) collective-permute-start(bf16[64,32,128]{2,1,0:T(8,128)(2,1)S(1)} %pad_maximum_fusion.1.refs_2_), channel_id=1, source_target_pairs={{0,1},{1,2},{2,3},{3,4},{4,5},{5,6},{6,7},{7,8},{8,9},{9,10},{10,1... | collective-permute-start | bytes 1572872 | tf_op jit(solution)/shard_map/ppermute | solution.py:28
  13.4 31.7 %collective-permute-start.4 = (bf16[64,32,128]{2,1,0:T(8,128)(2,1)S(1)}, bf16[64,32,128]{2,1,0:T(8,128)(2,1)}, u32[]{:S(2)}, u32[]{:S(2)}) collective-permute-start(bf16[64,32,128]{2,1,0:T(8,128)(2,1)S(1)} %pad_maximum_fusion.1.refs_2_), channel_id=1, source_target_pairs={{0,63},{1,0},{2,1},{3,2},{4,3},{5,4},{6,5},{7,6},{8,7},{9,8},{10,9... | collective-permute-start | bytes 1572872 | tf_op jit(solution)/shard_map/ppermute | solution.py:28
  20.5 23.1 %collective-permute-start.7 = (bf16[64,16,128]{2,1,0:T(8,128)(2,1)}, bf16[64,16,128]{2,1,0:T(8,128)(2,1)S(1)}, u32[]{:S(2)}, u32[]{:S(2)}) collective-permute-start(bf16[64,16,128]{2,1,0:T(8,128)(2,1)} %get-tuple-element.5), channel_id=1, source_target_pairs={{0,128},{128,0},{64,192},{192,64},{1,129},{129,1},{65,193},{193,65... | collective-permute-start | bytes 786440 | tf_op jit(solution)/shard_map/ppermute | solution.py:137
  43.6 9.5 %copy-start.2 = (bf16[64,16,128]{2,1,0:T(8,128)(2,1)}, bf16[64,16,128]{2,1,0:T(8,128)(2,1)S(1)}, u32[]{:S(2)}) copy-start(bf16[64,16,128]{2,1,0:T(8,128)(2,1)S(1)} %collective-permute-done.7.refs_7_) | copy-start | bytes 786436
  43.6 30.1 %collective-permute-start.10 = (bf16[64,16,128]{2,1,0:T(8,128)(2,1)S(1)}, bf16[64,16,128]{2,1,0:T(8,128)(2,1)}, u32[]{:S(2)}, u32[]{:S(2)}) collective-permute-start(bf16[64,16,128]{2,1,0:T(8,128)(2,1)S(1)} %collective-permute-done.7.refs_7_), channel_id=1, source_target_pairs={{0,63},{1,0},{2,1},{3,2},{4,3},{5,4},{6,5},{7,6},{8,7},{9,8},{10,9... | collective-permute-start | bytes 786440 | tf_op jit(solution)/shard_map/ppermute | solution.py:28
  44.4 30.2 %collective-permute-start.8 = (bf16[64,16,128]{2,1,0:T(8,128)(2,1)S(1)}, bf16[64,16,128]{2,1,0:T(8,128)(2,1)}, u32[]{:S(2)}, u32[]{:S(2)}) collective-permute-start(bf16[64,16,128]{2,1,0:T(8,128)(2,1)S(1)} %collective-permute-done.7.refs_7_), channel_id=1, source_target_pairs={{0,1},{1,2},{2,3},{3,4},{4,5},{5,6},{6,7},{7,8},{8,9},{9,10},{10,1... | collective-permute-start | bytes 786440 | tf_op jit(solution)/shard_map/ppermute | solution.py:28
  45.1 38.2 %collective-permute-start.3 = (bf16[64,32,128]{2,1,0:T(8,128)(2,1)}, bf16[64,32,128]{2,1,0:T(8,128)(2,1)}, u32[]{:S(2)}, u32[]{:S(2)}) collective-permute-start(bf16[64,32,128]{2,1,0:T(8,128)(2,1)} %collective-permute-done.2.refs_1_), channel_id=1, source_target_pairs={{0,1},{1,2},{2,3},{3,4},{4,5},{5,6},{6,7},{7,8},{8,9},{9,10},{10,1... | collective-permute-start | bytes 1572872 | tf_op jit(solution)/shard_map/ppermute | solution.py:28
  45.1 38.2 %collective-permute-start.5 = (bf16[64,32,128]{2,1,0:T(8,128)(2,1)}, bf16[64,32,128]{2,1,0:T(8,128)(2,1)}, u32[]{:S(2)}, u32[]{:S(2)}) collective-permute-start(bf16[64,32,128]{2,1,0:T(8,128)(2,1)} %collective-permute-done.4.refs_3_), channel_id=1, source_target_pairs={{0,63},{1,0},{2,1},{3,2},{4,3},{5,4},{6,5},{7,6},{8,7},{9,8},{10,9... | collective-permute-start | bytes 1572872 | tf_op jit(solution)/shard_map/ppermute | solution.py:28
  73.7 18.6 %collective-permute-start.11 = (bf16[64,16,128]{2,1,0:T(8,128)(2,1)}, bf16[64,16,128]{2,1,0:T(8,128)(2,1)}, u32[]{:S(2)}, u32[]{:S(2)}) collective-permute-start(bf16[64,16,128]{2,1,0:T(8,128)(2,1)} %collective-permute-done.10.refs_8_), channel_id=1, source_target_pairs={{0,63},{1,0},{2,1},{3,2},{4,3},{5,4},{6,5},{7,6},{8,7},{9,8},{10,9... | collective-permute-start | bytes 786440 | tf_op jit(solution)/shard_map/ppermute | solution.py:28
  74.6 17.8 %collective-permute-start.9 = (bf16[64,16,128]{2,1,0:T(8,128)(2,1)}, bf16[64,16,128]{2,1,0:T(8,128)(2,1)}, u32[]{:S(2)}, u32[]{:S(2)}) collective-permute-start(bf16[64,16,128]{2,1,0:T(8,128)(2,1)} %collective-permute-done.8.refs_6_), channel_id=1, source_target_pairs={{0,1},{1,2},{2,3},{3,4},{4,5},{5,6},{6,7},{7,8},{8,9},{9,10},{10,1... | collective-permute-start | bytes 786440 | tf_op jit(solution)/shard_map/ppermute | solution.py:28
  83.3 9.1 %copy-start.3 = (bf16[64,16,128]{2,1,0:T(8,128)(2,1)S(1)}, bf16[64,16,128]{2,1,0:T(8,128)(2,1)}, u32[]{:S(2)}) copy-start(bf16[64,16,128]{2,1,0:T(8,128)(2,1)} %copy-done.2) | copy-start | bytes 786436
  103.9 3.5 %collective-permute-start.12 = (bf16[16,64,128]{2,1,0:T(8,128)(2,1)S(1)}, bf16[16,64,128]{2,1,0:T(8,128)(2,1)S(1)}, u32[]{:S(2)}, u32[]{:S(2)}) collective-permute-start(bf16[16,64,128]{2,1,0:T(8,128)(2,1)S(1)} %bitcast.39), channel_id=1, source_target_pairs={{0,64},{64,0},{128,192},{192,128},{1,65},{65,1},{129,193},{193,129... | collective-permute-start | bytes 786440 | tf_op jit(solution)/shard_map/ppermute | solution.py:176
  (2 other events, 10.1 us)

commit v2 on v0

v2 whole, which is shorter than its diff:
```python
import functools

import jax
import jax.numpy as jnp
from jax import lax
from jax.experimental import pallas as pl
from jax.experimental.pallas import tpu as pltpu
from jax.sharding import PartitionSpec as P

K = 9
G = 8
R = 16
RG = 8
NB = 4
BW = 8
SMAX = 2
J = 2
T = BW + J - 1
SECTORS = 2 * SMAX + 1
PADDED = 384
VMEM = pl.BlockSpec(memory_space=pltpu.VMEM)
SMEM = pl.BlockSpec(memory_space=pltpu.SMEM)
ANY = pl.BlockSpec(memory_space=pl.ANY)


def send(value, across, core, steps):
    count = lax.axis_size("lon")
    pairs = []
    for lat in range(4):
        target = (lat ^ (2 * across)) ^ core
        for lon in range(count):
            pairs.append((lat * count + lon, target * count + (lon + steps) % count))
    return lax.ppermute(value, ("lat", "lon"), pairs)


def prep_kernel(place_ref, filt_ref, far_ref, near_ref, edge_ref, spread_ref, pick_ref, pick_edge_ref):
    upper = place_ref[0]
    far = place_ref[1]
    deep = NB * PADDED
    wide = BW * NB * 2 * R

    def fill(ref, target):
        width = ref.shape[1]

        def some(n, carry):
            row = n * 128 + lax.broadcasted_iota(jnp.int32, (128, width), 0)
            hit = jnp.where(row == target, 1.0, 0.0)
            ref[pl.ds(pl.multiple_of(n * 128, 128), 128), :] = hit.astype(jnp.bfloat16)
            return carry

        lax.fori_loop(0, deep // 128, some, 0)

    def own_target(start):
        c = lax.broadcasted_iota(jnp.int32, (1, wide), 1)
        return ((c >> 5) & 3) * PADDED + ((c & 31) + start) * BW + (c >> 7)

    def edge_target(start, j):
        c = lax.broadcasted_iota(jnp.int32, (1, T * NB * R), 1)
        t = (c >> 6) - j
        at = ((c >> 4) & 3) * PADDED + ((c & 15) + start) * BW + t
        return jnp.where((t >= 0) & (t < BW), at, -1)

    for j in range(J):
        fill(pick_edge_ref.at[j], edge_target(2 * R * (1 - upper), j))
    for which in range(2):
        half = jnp.where(far == 1, which, 1 - which)
        out_ref = (far_ref, near_ref)[which]
        fill(pick_ref, own_target(R * (1 - upper) if which == 0 else R * upper))
        for g in range(2):
            for p in range(RG):
                i = g * RG + p
                for b in range(NB):
                    x = filt_ref[half, i, b].astype(jnp.float32)
                    if i:
                        x = pltpu.roll(x, BW * i, 1)
                    for n in range(PADDED // 128):
                        at = b * PADDED // 128 + n
                        spread_ref[at, pl.ds(p, K, stride=RG), :] = x[:, n * 128 : (n + 1) * 128]
            spread = jnp.concatenate([spread_ref[n] for n in range(deep // 128)], axis=1)
            spread = spread.astype(jnp.bfloat16)
            own = jnp.dot(spread, pick_ref[...], preferred_element_type=jnp.float32)
            blank = jnp.zeros((RG, 128), jnp.float32)
            for k in range(K):
                rows = own[k * RG : (k + 1) * RG]
                first = jnp.concatenate([rows, blank], axis=1)
                second = jnp.concatenate([blank, rows], axis=1)
                both = jnp.concatenate([first, second], axis=0)
                out_ref[g, k * 16 : (k + 1) * 16, :] = both.astype(jnp.bfloat16)
            if which:
                edges = [
                    jnp.dot(spread, pick_edge_ref[j], preferred_element_type=jnp.float32)
                    for j in range(J)
                ]
                for k in range(K):
                    both = jnp.concatenate([e[k * RG : (k + 1) * RG] for e in edges], axis=0)
                    edge_ref[g, k * 16 : (k + 1) * 16, :] = both.astype(jnp.bfloat16)


def left_sides(place, filters):
    wide, edge, deep = T * NB * 2 * R, T * NB * R, NB * PADDED
    return pl.pallas_call(
        prep_kernel,
        out_shape=[
            jax.ShapeDtypeStruct((2, K * J * RG, width), jnp.bfloat16)
            for width in (wide, wide, edge)
        ],
        in_specs=[SMEM, VMEM],
        out_specs=[VMEM] * 3,
        scratch_shapes=[
            pltpu.VMEM((deep // 128, K * RG, 128), jnp.float32),
            pltpu.VMEM((deep, BW * NB * 2 * R), jnp.bfloat16),
            pltpu.VMEM((J, deep, edge), jnp.bfloat16),
        ],
        compiler_params=pltpu.CompilerParams(vmem_limit_bytes=24 << 20),
        cost_estimate=pl.CostEstimate(flops=8 * 10**9, bytes_accessed=4 << 20, transcendentals=0),
    )(place, filters)


def fetch(place_ref, pieces, ext_ref, sems):
    lon = pieces[0].shape[0]
    copies = []
    for n, piece in enumerate(pieces):
        row_set, sector = n // SECTORS, n % SECTORS
        target = ext_ref.at[pl.ds(sector * lon, lon)]
        if len(pieces) > SECTORS:
            core = place_ref[2]
            first = jnp.where(core == row_set, 0, R)
            target = ext_ref.at[pl.ds(sector * lon, lon), pl.ds(pl.multiple_of(first, R), R)]
        copies.append(pltpu.make_async_copy(piece, target, sems.at[n]))
    for copy in copies:
        copy.start()
    for copy in copies:
        copy.wait()


def product(left, ext_ref, shift_ref, g, jb, lon):
    columns = []
    for side in range(2):
        at = SMAX * lon + jb * J + side * (lon // 2)
        starts = [at + shift_ref[g, b] for b in range(NB)]
        rows = [ext_ref[starts[b] + t] for t in range(T) for b in range(NB)]
        columns.append(jnp.concatenate(rows, axis=0))
    right = jnp.concatenate(columns, axis=1)
    return jnp.dot(left, right, preferred_element_type=jnp.float32)


def keep(resp_ref, resp, jb):
    resp = resp.astype(jnp.bfloat16)
    width = resp.shape[1]
    rows = pl.ds(pl.multiple_of(jb * 16, 16), 16)
    for k in range(K):
        resp_ref[rows, k * width : (k + 1) * width] = resp[k * 16 : (k + 1) * 16]


def mix_rows(resp_ref, mix_ref, mixed_ref, out_ref, g):
    mixed = jnp.dot(resp_ref[...], mix_ref[...], preferred_element_type=jnp.float32)
    chans = mixed.shape[1] // 2
    half = mixed.shape[0] // RG
    for side in range(2):
        mixed_ref[side] = mixed[:, side * chans : (side + 1) * chans]
        for p in range(RG):
            rows = mixed_ref[side, pl.ds(p, half, stride=RG), :]
            out_ref[g, p, side * half : (side + 1) * half, :] = rows.astype(jnp.bfloat16)


def over_groups(steps, step, after):
    def group(g, carry):
        def one(jb, carry):
            step(g, jb)
            return carry

        lax.fori_loop(0, steps, one, 0, unroll=True)
        after(g)
        return carry

    lax.fori_loop(0, 2, group, 0)


def far_kernel(place_ref, shift_ref, *refs):
    pieces = refs[: 2 * SECTORS]
    left_ref, mix_ref, out_ref, ext_ref, resp_ref, mixed_ref, sems = refs[2 * SECTORS :]
    lon = pieces[0].shape[0]
    fetch(place_ref, pieces, ext_ref, sems)
    over_groups(
        lon // 2 // J,
        lambda g, jb: keep(resp_ref, product(left_ref[g], ext_ref, shift_ref, g, jb, lon), jb),
        lambda g: mix_rows(resp_ref, mix_ref, mixed_ref, out_ref, g),
    )


def near_kernel(place_ref, shift_ref, *refs):
    pieces = refs[: 2 * SECTORS]
    left_ref, sums_ref, ext_ref, sems = refs[2 * SECTORS :]
    lon = pieces[0].shape[0]
    fetch(place_ref, pieces, ext_ref, sems)

    def step(g, jb):
        sums_ref[g, jb] = product(left_ref[g], ext_ref, shift_ref, g, jb, lon)

    over_groups(lon // 2 // J, step, lambda g: None)


def edge_kernel(place_ref, shift_ref, *refs):
    pieces = refs[:SECTORS]
    left_ref, mix_ref, sums_ref, out_ref, ext_ref, resp_ref, mixed_ref, sems = refs[SECTORS:]
    lon = pieces[0].shape[0]
    fetch(place_ref, pieces, ext_ref, sems)

    def step(g, jb):
        resp = sums_ref[g, jb] + product(left_ref[g], ext_ref, shift_ref, g, jb, lon)
        keep(resp_ref, resp, jb)

    over_groups(
        lon // 2 // J, step, lambda g: mix_rows(resp_ref, mix_ref, mixed_ref, out_ref, g)
    )


def conv(kernel, place, shifts, pieces, left, mix=None, sums=None):
    lon, _, chans = pieces[0].shape
    depth = R * (len(pieces) // SECTORS)
    half = lon // 2
    ext = [pltpu.VMEM((SECTORS * lon, depth, chans), jnp.bfloat16)]
    sems = [pltpu.SemaphoreType.DMA((len(pieces),))]
    if mix is None:
        out = jax.ShapeDtypeStruct((2, half // J, K * J * RG, 2 * chans), jnp.float32)
        scratch = ext + sems
    else:
        out = jax.ShapeDtypeStruct((2, RG, lon, chans), jnp.bfloat16)
        scratch = ext + [
            pltpu.VMEM((half * RG, K * 2 * chans), jnp.bfloat16),
            pltpu.VMEM((2, half * RG, chans), jnp.float32),
        ]
        scratch += sems
    arrays = [left] + [x for x in (mix, sums) if x is not None]
    return pl.pallas_call(
        kernel,
        out_shape=out,
        in_specs=[SMEM, SMEM] + [ANY] * len(pieces) + [VMEM] * len(arrays),
        out_specs=VMEM,
        scratch_shapes=scratch,
        compiler_params=pltpu.CompilerParams(vmem_limit_bytes=24 << 20),
        cost_estimate=pl.CostEstimate(
            flops=4 * left.size * half // J * 2 * chans, bytes_accessed=8 << 20, transcendentals=0
        ),
    )(place, shifts, *pieces, *arrays)


def after(value, *others):
    return lax.optimization_barrier((value, *others))[0]


def on_device(field, filters, sector_width, block_offset, mixing):
    rows, lon, chans = field.shape
    half = chans // 2
    lat = lax.axis_index("lat")
    upper, core = lat // 2, lat % 2
    first = core == 0
    far = core == upper
    place = jnp.stack([upper, far.astype(jnp.int32), core]).astype(jnp.int32)

    turned = field.transpose(1, 0, 2)
    low, high = turned[:, :, :half], turned[:, :, half:]
    mine, theirs = lax.optimization_barrier(
        (jnp.where(first, low, high), jnp.where(first, high, low))
    )
    got = send(theirs, 0, 1, 0)
    mine_w, mine_e = send(mine, 0, 0, 1), send(mine, 0, 0, -1)
    got_w, got_e = send(theirs, 0, 1, 1), send(theirs, 0, 1, -1)

    shifts = BW * block_offset * sector_width[:, None]
    filters = after(filters, mine)
    other_shifts = send(after(shifts, mine), 0, 1, 0)
    other_filters = send(filters, 0, 1, 0)
    far_shifts = jnp.where(far, shifts, other_shifts)
    near_shifts = jnp.where(far, other_shifts, shifts)
    both = jnp.stack([filters, other_filters])
    both = jnp.pad(both, ((0, 0),) * 4 + ((0, PADDED - both.shape[-1]),))
    far_left, near_left, edge_left = left_sides(place, both)

    group_chans = chans // G
    side = lax.dynamic_slice_in_dim(after(mixing, mine), core * half, half, axis=2)
    tiled = jnp.tile(side, (1, chans // group_chans, 2))
    row_at = lax.broadcasted_iota(jnp.int32, (chans, chans), 0) // group_chans
    col_at = lax.broadcasted_iota(jnp.int32, (chans, chans), 1) // group_chans
    mix = jnp.where((row_at == col_at)[None], tiled, jnp.zeros_like(tiled))
    mix = mix.reshape(K * chans, chans)

    edge = send(jnp.where(far, got, mine), 1, 0, 0)

    mine_w2, mine_e2 = send(mine_w, 0, 0, 1), send(mine_e, 0, 0, -1)
    got_w2, got_e2 = send(got_w, 0, 0, 1), send(got_e, 0, 0, -1)
    pieces = [mine_w2, mine_w, mine, mine_e, mine_e2, got_w2, got_w, got, got_e, got_e2]
    pieces = list(lax.optimization_barrier(tuple(pieces)))
    edge = after(edge, *pieces)
    edge_w, edge_e = send(edge, 0, 0, 1), send(edge, 0, 0, -1)
    sums = conv(near_kernel, place, near_shifts, pieces, near_left)
    edge_w, edge_e, sums = lax.optimization_barrier((edge_w, edge_e, sums))
    edge_w2, edge_e2 = send(edge_w, 0, 0, 1), send(edge_e, 0, 0, -1)
    pieces = list(lax.optimization_barrier((*pieces, sums))[:-1])
    far_out = conv(far_kernel, place, far_shifts, pieces, far_left, mix)
    edges = [edge_w2, edge_w, edge, edge_e, edge_e2]
    edges, far_out = lax.optimization_barrier((edges, far_out))
    near_out = conv(edge_kernel, place, near_shifts, edges, edge_left, mix, sums)

    far_out, near_out = (x.reshape(rows, lon, half) for x in (far_out, near_out))
    kept = jnp.where(far, far_out, near_out)
    other = send(jnp.where(far, near_out, far_out), 0, 1, 0)
    return jnp.concatenate([jnp.where(first, kept, other), jnp.where(first, other, kept)], axis=2)


def solution(mesh):
    return jax.shard_map(
        on_device,
        mesh=mesh,
        in_specs=(P("lat", "lon", None), P("lat", None, None, None), P("lat"), P("lat", None), P()),
        out_specs=P("lat", "lon", None),
        check_vma=False,
    )
```

time: 321 us -> 77.5 us (0.24)
  local copies, waits for them, and re-layouts: 111 us -> 2.9 us
  matrix products: 77.9 us -> 0 us
  waiting for transfers between devices: 76.7 us -> 14.9 us
  Pallas kernels: 0 us -> 19.8 us
  loops' own time: 10.1 us -> 0 us
  starting transfers between devices: 41.7 us -> 37.6 us
    dot_general x34 -> x0, matrix products: 77.9 us -> none  [the longest x8 72.2 us: process_group(): jnp.dot(left_side, stacked, preferred_element_type=jnp.float32)]
    while x24 -> x0, local copies, waits for them, and re-layouts: 67.6 us -> none
    ppermute x6 -> x17, waiting for transfers between devices: 76.7 us -> 14.9 us  [send(): return lax.ppermute(value, ('lat', 'lon'), pairs)]
    pallas_call x0 -> x4, Pallas kernels: none -> 19.8 us  [the longest x3 13.3 us: conv(): pl.pallas_call(kernel, out_shape=out, in_specs=[SMEM, SMEM] + [ANY] * len...]
    concatenate x6 -> x0, local copies, waits for them, and re-layouts: 19.2 us -> none  [the longest x4 18.3 us: process_group(): jnp.concatenate([window[:, column * chans:(column + lon_dev) * chans] for...]
    another operation x1 -> x0, loops' own time: 10.1 us -> none  [on_device(): results = lax.map(process_group, jnp.arange(groups, dtype=jnp.int32))]
    reshape x16 -> x0, local copies, waits for them, and re-layouts: 9 us -> none  [process_group(): group_filters[:, block_index].astype(jnp.float32).reshape(RG, K, span, BW)]
    unnamed x17 -> x9, local copies, waits for them, and re-layouts: 7.92 us -> 1.41 us
  transfers between devices with their start and end apart: 6 -> 17, of which waited for: 5 -> 5; matrix products, arithmetic and copies ran while one was open for 2% -> 3% of each run, Pallas kernels for 0% -> 21%
where the time goes in v2:
time: 77.5 us; the launch traced here: 77.4 us
  starting transfers between devices  37.6 us (49%)
  Pallas kernels  19.8 us (26%)
  waiting for transfers between devices  14.9 us (19%)
  local copies, waits for them, and re-layouts  2.9 us (4%)
  other arithmetic  1.98 us (3%)
    ppermute x17, starting transfers between devices, send(): return lax.ppermute(value, ('lat', 'lon'), pairs)  37.6 us
    ppermute x17, waiting for transfers between devices, send(): return lax.ppermute(value, ('lat', 'lon'), pairs)  14.9 us
    pallas_call x3, Pallas kernels, conv(): pl.pallas_call(kernel, out_shape=out, in_specs=[SMEM, SMEM] + [ANY] * len...  13.3 us
    pallas_call x1, Pallas kernels, left_sides(): pl.pallas_call(prep_kernel, out_shape=[jax.ShapeDtypeStruct((2, K * J * R...  6.55 us
  transfers between devices with their start and end apart: 17, of which 5 were waited for; matrix products, arithmetic and copies ran while one was open for 3% of the time, Pallas kernels for 21%

profile of v2, /device:TPU:1, one launch (start us, length us, event | category | flops | bytes accessed | tf_op | source)
XLA Modules:
  0.0 77.4 jit_solution(16141856383347975466)
XLA Ops:
  0.0 1.4 %copy.20 = bf16[16,64,256]{2,0,1:T(8,128)(2,1)S(1)} copy(bf16[16,64,256]{2,1,0:T(8,128)(2,1)} %param.5) | data formatting | bytes 1048576 | tf_op args[0]
  1.5 10.2 %collective-permute-start.8 = (bf16[64,16,128]{2,1,0:T(8,128)(2,1)S(1)}, bf16[64,16,128]{2,1,0:T(8,128)(2,1)S(1)}, u32[]{:S(2)}, u32[]{:S(2)}) collective-permute-start(bf16[64,16,128]{2,1,0:T(8,128)(2,1)S(1)} %get-tuple-element.43), channel_id=1, source_target_pairs={{0,127},{1,64},{2,65},{3,66},{4,67},{5,68},{6,69},{7,70},{8,71},{9... | collective-permute-start | bytes 786440 | tf_op jit(solution)/shard_map/ppermute | solution.py:33
  11.7 6.1 %collective-permute-start.4 = (bf16[64,16,128]{2,1,0:T(8,128)(2,1)S(1)}, bf16[64,16,128]{2,1,0:T(8,128)(2,1)S(1)}, u32[]{:S(2)}, u32[]{:S(2)}) collective-permute-start(bf16[64,16,128]{2,1,0:T(8,128)(2,1)S(1)} %get-tuple-element.64.refs_2_), channel_id=1, source_target_pairs={{0,63},{1,0},{2,1},{3,2},{4,3},{5,4},{6,5},{7,6},{8,7},{9,8},{10,9... | collective-permute-start | bytes 786440 | tf_op jit(solution)/shard_map/ppermute | solution.py:33
  17.9 0.3 collective-permute-start.12
  18.7 1.1 %tile.4 = bf16[9,8,32,2,128]{4,3,2,1,0:T(2,128)(2,1)S(1)} broadcast(bf16[9,32,128]{2,1,0:T(8,128)(2,1)S(1)} %constant_dynamic-slice_fusion), dimensions={0,2,4} | broadcast | bytes 1253376 | tf_op jit(solution)/shard_map/tile | solution.py:282
  19.8 0.2 bitcast_select_fusion.refs_11_.refs_6_
  20.1 0.3 collective-permute-start.13
  20.6 2.7 %collective-permute-start.1 = (bf16[64,16,128]{2,1,0:T(8,128)(2,1)S(1)}, bf16[64,16,128]{2,1,0:T(8,128)(2,1)S(1)}, u32[]{:S(2)}, u32[]{:S(2)}) collective-permute-start(bf16[64,16,128]{2,1,0:T(8,128)(2,1)S(1)} %broadcast_select_fusion.2), channel_id=1, source_target_pairs={{0,128},{1,129},{2,130},{3,131},{4,132},{5,133},{6,134},{7,135},{8... | collective-permute-start | bytes 786440 | tf_op jit(solution)/shard_map/ppermute | solution.py:33
  23.3 0.5 collective-permute-done.6.refs_6_
  23.8 4.7 %collective-permute-start.9 = (bf16[64,16,128]{2,1,0:T(8,128)(2,1)S(1)}, bf16[64,16,128]{2,1,0:T(8,128)(2,1)S(1)}, u32[]{:S(2)}, u32[]{:S(2)}) collective-permute-start(bf16[64,16,128]{2,1,0:T(8,128)(2,1)S(1)} %collective-permute-done.8.refs_8_), channel_id=1, source_target_pairs={{0,63},{1,0},{2,1},{3,2},{4,3},{5,4},{6,5},{7,6},{8,7},{9,8},{10,9... | collective-permute-start | bytes 786440 | tf_op jit(solution)/shard_map/ppermute | solution.py:33
  28.5 3.5 %collective-permute-done.2.refs_1_ = bf16[64,16,128]{2,1,0:T(8,128)(2,1)S(1)} collective-permute-done((bf16[64,16,128]{2,1,0:T(8,128)(2,1)S(1)}, bf16[64,16,128]{2,1,0:T(8,128)(2,1)S(1)}, u32[]{:S(2)}, u32[]{:S(2)}) %collective-permute-start.2) | collective-permute-done | bytes 262176 | tf_op jit(solution)/shard_map/ppermute | solution.py:33
  32.0 2.2 %collective-permute-start.5 = (bf16[64,16,128]{2,1,0:T(8,128)(2,1)S(1)}, bf16[64,16,128]{2,1,0:T(8,128)(2,1)S(1)}, u32[]{:S(2)}, u32[]{:S(2)}) collective-permute-start(bf16[64,16,128]{2,1,0:T(8,128)(2,1)S(1)} %collective-permute-done.4.refs_3_), channel_id=1, source_target_pairs={{0,63},{1,0},{2,1},{3,2},{4,3},{5,4},{6,5},{7,6},{8,7},{9,8},{10,9... | collective-permute-start | bytes 786440 | tf_op jit(solution)/shard_map/ppermute | solution.py:33
  34.4 0.4 fusion.2.filt_ref
  34.8 6.5 %shard_map.55 = (bf16[2,144,1152]{2,1,0:T(8,128)(2,1)S(1)}, bf16[2,144,1152]{2,1,0:T(8,128)(2,1)S(1)}, bf16[2,144,576]{2,1,0:T(8,128)(2,1)S(1)}) custom-call(s32[3]{0:T(128)S(1)} %pad_add_fusion.place_ref, bf16[2,16,4,9,384]{4,3,2,1,0:T(8,128)(2,1)S(1)} %fusion.2.filt_ref), custom_call_target="tpu_custom_call" | custom-call | flops 8000000000 | bytes 4194304 | tf_op jit(solution)/shard_map/pallas_call | solution.py:101
  41.3 3.8 %collective-permute-done.3.refs_0_ = bf16[64,16,128]{2,1,0:T(8,128)(2,1)S(1)} collective-permute-done((bf16[64,16,128]{2,1,0:T(8,128)(2,1)S(1)}, bf16[64,16,128]{2,1,0:T(8,128)(2,1)S(1)}, u32[]{:S(2)}, u32[]{:S(2)}) %collective-permute-start.3) | collective-permute-done | bytes 262176 | tf_op jit(solution)/shard_map/ppermute | solution.py:33
  45.1 2.0 %collective-permute-start.11 = (bf16[64,16,128]{2,1,0:T(8,128)(2,1)S(1)}, bf16[64,16,128]{2,1,0:T(8,128)(2,1)S(1)}, u32[]{:S(2)}, u32[]{:S(2)}) collective-permute-start(bf16[64,16,128]{2,1,0:T(8,128)(2,1)S(1)} %collective-permute-done.1.refs_2_), channel_id=1, source_target_pairs={{0,63},{1,0},{2,1},{3,2},{4,3},{5,4},{6,5},{7,6},{8,7},{9,8},{10,9... | collective-permute-start | bytes 786440 | tf_op jit(solution)/shard_map/ppermute | solution.py:33
  47.1 4.4 %shard_map.56.refs_7_ = f32[2,16,144,256]{3,2,1,0:T(8,128)S(1)} custom-call(s32[3]{0:T(128)S(1)} %pad_add_fusion.place_ref, s32[2,4]{1,0:T(2,128)S(1)} %get-tuple-element.88.shift_ref, bf16[64,16,128]{2,1,0:T(8,128)(2,1)S(1)} %collective-permute-done.3.refs_0_, bf16[64,16,128]{2,1,0:T(8,128)(2,1)S(1)} %collective-permute-done.2.refs_1_, ...), custom_call_target="tpu_custom_call" | custom-call | flops 5435817984 | bytes 8388608 | tf_op jit(solution)/shard_map/pallas_call | solution.py:235
  51.6 5.9 %collective-permute-done.10.refs_1_ = bf16[64,16,128]{2,1,0:T(8,128)(2,1)S(1)} collective-permute-done((bf16[64,16,128]{2,1,0:T(8,128)(2,1)S(1)}, bf16[64,16,128]{2,1,0:T(8,128)(2,1)S(1)}, u32[]{:S(2)}, u32[]{:S(2)}) %collective-permute-start.10) | collective-permute-done | bytes 262176 | tf_op jit(solution)/shard_map/ppermute | solution.py:33
  57.5 5.7 %collective-permute-start.15 = (bf16[64,16,128]{2,1,0:T(8,128)(2,1)S(1)}, bf16[64,16,128]{2,1,0:T(8,128)(2,1)S(1)}, u32[]{:S(2)}, u32[]{:S(2)}) collective-permute-start(bf16[64,16,128]{2,1,0:T(8,128)(2,1)S(1)} %collective-permute-done.11.refs_3_), channel_id=1, source_target_pairs={{0,63},{1,0},{2,1},{3,2},{4,3},{5,4},{6,5},{7,6},{8,7},{9,8},{10,9... | collective-permute-start | bytes 786440 | tf_op jit(solution)/shard_map/ppermute | solution.py:33
  63.1 5.2 %shard_map.57 = bf16[2,8,64,128]{3,2,1,0:T(8,128)(2,1)S(1)} custom-call(s32[3]{0:T(128)S(1)} %pad_add_fusion.place_ref, s32[2,4]{1,0:T(2,128)S(1)} %get-tuple-element.87.shift_ref, bf16[64,16,128]{2,1,0:T(8,128)(2,1)S(1)} %collective-permute-done.3.refs_0_, bf16[64,16,128]{2,1,0:T(8,128)(2,1)S(1)} %collective-permute-done.2.refs_1_, ...), custom_call_target="tpu_custom_call" | custom-call | flops 5435817984 | bytes 8388608 | tf_op jit(solution)/shard_map/pallas_call | solution.py:235
  68.4 3.6 %shard_map.58 = bf16[2,8,64,128]{3,2,1,0:T(8,128)(2,1)S(1)} custom-call(s32[3]{0:T(128)S(1)} %pad_add_fusion.place_ref, s32[2,4]{1,0:T(2,128)S(1)} %get-tuple-element.88.shift_ref, bf16[64,16,128]{2,1,0:T(8,128)(2,1)S(1)} %collective-permute-done.14.refs_0_, bf16[64,16,128]{2,1,0:T(8,128)(2,1)S(1)} %collective-permute-done.10.refs_1_, ...), custom_call_target="tpu_custom_call" | custom-call | flops 2717908992 | bytes 8388608 | tf_op jit(solution)/shard_map/pallas_call | solution.py:235
  72.1 3.3 %collective-permute-start.16 = (bf16[16,64,128]{2,1,0:T(8,128)(2,1)S(1)}, bf16[16,64,128]{2,1,0:T(8,128)(2,1)S(1)}, u32[]{:S(2)}, u32[]{:S(2)}) collective-permute-start(bf16[16,64,128]{2,1,0:T(8,128)(2,1)S(1)} %bitcast.26), channel_id=1, source_target_pairs={{0,64},{1,65},{2,66},{3,67},{4,68},{5,69},{6,70},{7,71},{8,72},{9,... | collective-permute-start | bytes 786440 | tf_op jit(solution)/shard_map/ppermute | solution.py:33
  75.3 1.2 %collective-permute-done.16 = bf16[16,64,128]{2,1,0:T(8,128)(2,1)S(1)} collective-permute-done((bf16[16,64,128]{2,1,0:T(8,128)(2,1)S(1)}, bf16[16,64,128]{2,1,0:T(8,128)(2,1)S(1)}, u32[]{:S(2)}, u32[]{:S(2)}) %collective-permute-start.16) | collective-permute-done | bytes 262176 | tf_op jit(solution)/shard_map/ppermute | solution.py:33
  76.5 0.9 %pad_maximum_fusion = bf16[16,64,256]{2,1,0:T(8,128)(2,1)} fusion(bf16[16,64,128]{2,1,0:T(8,128)(2,1)S(1)} %get-tuple-element.82, bf16[16,64,128]{2,1,0:T(8,128)(2,1)S(1)} %get-tuple-element.81), kind=kLoop, calls=%fused_computation.7 | loop fusion | flops 1048576 | bytes 1048576 | tf_op jit(solution)/shard_map/concatenate | solution.py:308
  (42 shorter events, 1.0 us)
Async XLA Ops:
  0.0 18.6 %copy-start = (bf16[9,32,256]{2,1,0:T(8,128)(2,1)S(1)}, bf16[9,32,256]{2,1,0:T(8,128)(2,1)}, u32[]{:S(2)}) copy-start(bf16[9,32,256]{2,1,0:T(8,128)(2,1)} %param.9) | copy-start | bytes 442372
  0.0 17.8 %copy-start.3 = (s32[2]{0:T(128)S(1)}, s32[2]{0:T(128)}, u32[]{:S(2)}) copy-start(s32[2]{0:T(128)} %param.7) | copy-start | bytes 28
  0.0 17.8 %copy-start.2 = (s32[2,4]{1,0:T(2,128)S(1)}, s32[2,4]{1,0:T(2,128)}, u32[]{:S(2)}) copy-start(s32[2,4]{1,0:T(2,128)} %param.8) | copy-start | bytes 100
  0.0 18.4 %copy-start.1 = (bf16[16,4,9,264]{3,1,2,0:T(4,128)(2,1)S(1)}, bf16[16,4,9,264]{3,1,2,0:T(4,128)(2,1)}, u32[]{:S(2)}) copy-start(bf16[16,4,9,264]{3,1,2,0:T(4,128)(2,1)} %param.6) | copy-start | bytes 912388
  1.5 19.1 %collective-permute-start.8 = (bf16[64,16,128]{2,1,0:T(8,128)(2,1)S(1)}, bf16[64,16,128]{2,1,0:T(8,128)(2,1)S(1)}, u32[]{:S(2)}, u32[]{:S(2)}) collective-permute-start(bf16[64,16,128]{2,1,0:T(8,128)(2,1)S(1)} %get-tuple-element.43), channel_id=1, source_target_pairs={{0,127},{1,64},{2,65},{3,66},{4,67},{5,68},{6,69},{7,70},{8,71},{9... | collective-permute-start | bytes 786440 | tf_op jit(solution)/shard_map/ppermute | solution.py:33
  11.7 12.1 %collective-permute-start.6 = (bf16[64,16,128]{2,1,0:T(8,128)(2,1)S(1)}, bf16[64,16,128]{2,1,0:T(8,128)(2,1)S(1)}, u32[]{:S(2)}, u32[]{:S(2)}) collective-permute-start(bf16[64,16,128]{2,1,0:T(8,128)(2,1)S(1)} %get-tuple-element.43), channel_id=1, source_target_pairs={{0,65},{1,66},{2,67},{3,68},{4,69},{5,70},{6,71},{7,72},{8,73},{9,... | collective-permute-start | bytes 786440 | tf_op jit(solution)/shard_map/ppermute | solution.py:33
  11.7 8.4 %collective-permute-start = (bf16[64,16,128]{2,1,0:T(8,128)(2,1)S(1)}, bf16[64,16,128]{2,1,0:T(8,128)(2,1)S(1)}, u32[]{:S(2)}, u32[]{:S(2)}) collective-permute-start(bf16[64,16,128]{2,1,0:T(8,128)(2,1)S(1)} %get-tuple-element.43), channel_id=1, source_target_pairs={{0,64},{1,65},{2,66},{3,67},{4,68},{5,69},{6,70},{7,71},{8,72},{9,... | collective-permute-start | bytes 786440 | tf_op jit(solution)/shard_map/ppermute | solution.py:33
  11.7 16.8 %collective-permute-start.4 = (bf16[64,16,128]{2,1,0:T(8,128)(2,1)S(1)}, bf16[64,16,128]{2,1,0:T(8,128)(2,1)S(1)}, u32[]{:S(2)}, u32[]{:S(2)}) collective-permute-start(bf16[64,16,128]{2,1,0:T(8,128)(2,1)S(1)} %get-tuple-element.64.refs_2_), channel_id=1, source_target_pairs={{0,63},{1,0},{2,1},{3,2},{4,3},{5,4},{6,5},{7,6},{8,7},{9,8},{10,9... | collective-permute-start | bytes 786440 | tf_op jit(solution)/shard_map/ppermute | solution.py:33
  17.9 2.2 %collective-permute-start.12 = (s32[2,4]{1,0:T(2,128)S(1)}, s32[2,4]{1,0:T(2,128)S(1)}, u32[]{:S(2)}, u32[]{:S(2)}) collective-permute-start(s32[2,4]{1,0:T(2,128)S(1)} %broadcast_multiply_fusion), channel_id=1, source_target_pairs={{0,64},{1,65},{2,66},{3,67},{4,68},{5,69},{6,70},{7,71},{8,72},{9,... | collective-permute-start | bytes 104 | tf_op jit(solution)/shard_map/ppermute | solution.py:33
  20.1 11.9 %collective-permute-start.2 = (bf16[64,16,128]{2,1,0:T(8,128)(2,1)S(1)}, bf16[64,16,128]{2,1,0:T(8,128)(2,1)S(1)}, u32[]{:S(2)}, u32[]{:S(2)}) collective-permute-start(bf16[64,16,128]{2,1,0:T(8,128)(2,1)S(1)} %get-tuple-element.64.refs_2_), channel_id=1, source_target_pairs={{0,1},{1,2},{2,3},{3,4},{4,5},{5,6},{6,7},{7,8},{8,9},{9,10},{10,1... | collective-permute-start | bytes 786440 | tf_op jit(solution)/shard_map/ppermute | solution.py:33
  20.1 14.1 %collective-permute-start.13 = (bf16[16,4,9,264]{3,0,2,1:T(8,128)(2,1)S(1)}, bf16[16,4,9,264]{3,0,2,1:T(8,128)(2,1)S(1)}, u32[]{:S(2)}, u32[]{:S(2)}) collective-permute-start(bf16[16,4,9,264]{3,0,2,1:T(8,128)(2,1)S(1)} %copy.11), channel_id=1, source_target_pairs={{0,64},{1,65},{2,66},{3,67},{4,68},{5,69},{6,70},{7,71},{8,72},{9,... | collective-permute-start | bytes 912392 | tf_op jit(solution)/shard_map/ppermute | solution.py:33
  20.6 24.6 %collective-permute-start.1 = (bf16[64,16,128]{2,1,0:T(8,128)(2,1)S(1)}, bf16[64,16,128]{2,1,0:T(8,128)(2,1)S(1)}, u32[]{:S(2)}, u32[]{:S(2)}) collective-permute-start(bf16[64,16,128]{2,1,0:T(8,128)(2,1)S(1)} %broadcast_select_fusion.2), channel_id=1, source_target_pairs={{0,128},{1,129},{2,130},{3,131},{4,132},{5,133},{6,134},{7,135},{8... | collective-permute-start | bytes 786440 | tf_op jit(solution)/shard_map/ppermute | solution.py:33
  23.8 17.5 %collective-permute-start.9 = (bf16[64,16,128]{2,1,0:T(8,128)(2,1)S(1)}, bf16[64,16,128]{2,1,0:T(8,128)(2,1)S(1)}, u32[]{:S(2)}, u32[]{:S(2)}) collective-permute-start(bf16[64,16,128]{2,1,0:T(8,128)(2,1)S(1)} %collective-permute-done.8.refs_8_), channel_id=1, source_target_pairs={{0,63},{1,0},{2,1},{3,2},{4,3},{5,4},{6,5},{7,6},{8,7},{9,8},{10,9... | collective-permute-start | bytes 786440 | tf_op jit(solution)/shard_map/ppermute | solution.py:33
  28.5 12.8 %collective-permute-start.7 = (bf16[64,16,128]{2,1,0:T(8,128)(2,1)S(1)}, bf16[64,16,128]{2,1,0:T(8,128)(2,1)S(1)}, u32[]{:S(2)}, u32[]{:S(2)}) collective-permute-start(bf16[64,16,128]{2,1,0:T(8,128)(2,1)S(1)} %collective-permute-done.6.refs_6_), channel_id=1, source_target_pairs={{0,1},{1,2},{2,3},{3,4},{4,5},{5,6},{6,7},{7,8},{8,9},{9,10},{10,1... | collective-permute-start | bytes 786440 | tf_op jit(solution)/shard_map/ppermute | solution.py:33
  32.0 9.3 %collective-permute-start.5 = (bf16[64,16,128]{2,1,0:T(8,128)(2,1)S(1)}, bf16[64,16,128]{2,1,0:T(8,128)(2,1)S(1)}, u32[]{:S(2)}, u32[]{:S(2)}) collective-permute-start(bf16[64,16,128]{2,1,0:T(8,128)(2,1)S(1)} %collective-permute-done.4.refs_3_), channel_id=1, source_target_pairs={{0,63},{1,0},{2,1},{3,2},{4,3},{5,4},{6,5},{7,6},{8,7},{9,8},{10,9... | collective-permute-start | bytes 786440 | tf_op jit(solution)/shard_map/ppermute | solution.py:33
  34.2 10.9 %collective-permute-start.3 = (bf16[64,16,128]{2,1,0:T(8,128)(2,1)S(1)}, bf16[64,16,128]{2,1,0:T(8,128)(2,1)S(1)}, u32[]{:S(2)}, u32[]{:S(2)}) collective-permute-start(bf16[64,16,128]{2,1,0:T(8,128)(2,1)S(1)} %collective-permute-done.2.refs_1_), channel_id=1, source_target_pairs={{0,1},{1,2},{2,3},{3,4},{4,5},{5,6},{6,7},{7,8},{8,9},{9,10},{10,1... | collective-permute-start | bytes 786440 | tf_op jit(solution)/shard_map/ppermute | solution.py:33
  45.1 6.4 %collective-permute-start.11 = (bf16[64,16,128]{2,1,0:T(8,128)(2,1)S(1)}, bf16[64,16,128]{2,1,0:T(8,128)(2,1)S(1)}, u32[]{:S(2)}, u32[]{:S(2)}) collective-permute-start(bf16[64,16,128]{2,1,0:T(8,128)(2,1)S(1)} %collective-permute-done.1.refs_2_), channel_id=1, source_target_pairs={{0,63},{1,0},{2,1},{3,2},{4,3},{5,4},{6,5},{7,6},{8,7},{9,8},{10,9... | collective-permute-start | bytes 786440 | tf_op jit(solution)/shard_map/ppermute | solution.py:33
  47.1 10.3 %collective-permute-start.10 = (bf16[64,16,128]{2,1,0:T(8,128)(2,1)S(1)}, bf16[64,16,128]{2,1,0:T(8,128)(2,1)S(1)}, u32[]{:S(2)}, u32[]{:S(2)}) collective-permute-start(bf16[64,16,128]{2,1,0:T(8,128)(2,1)S(1)} %collective-permute-done.1.refs_2_), channel_id=1, source_target_pairs={{0,1},{1,2},{2,3},{3,4},{4,5},{5,6},{6,7},{7,8},{8,9},{9,10},{10,1... | collective-permute-start | bytes 786440 | tf_op jit(solution)/shard_map/ppermute | solution.py:33
  57.5 10.9 %collective-permute-start.14 = (bf16[64,16,128]{2,1,0:T(8,128)(2,1)S(1)}, bf16[64,16,128]{2,1,0:T(8,128)(2,1)S(1)}, u32[]{:S(2)}, u32[]{:S(2)}) collective-permute-start(bf16[64,16,128]{2,1,0:T(8,128)(2,1)S(1)} %collective-permute-done.10.refs_1_), channel_id=1, source_target_pairs={{0,1},{1,2},{2,3},{3,4},{4,5},{5,6},{6,7},{7,8},{8,9},{9,10},{10,1... | collective-permute-start | bytes 786440 | tf_op jit(solution)/shard_map/ppermute | solution.py:33
  57.5 10.9 %collective-permute-start.15 = (bf16[64,16,128]{2,1,0:T(8,128)(2,1)S(1)}, bf16[64,16,128]{2,1,0:T(8,128)(2,1)S(1)}, u32[]{:S(2)}, u32[]{:S(2)}) collective-permute-start(bf16[64,16,128]{2,1,0:T(8,128)(2,1)S(1)} %collective-permute-done.11.refs_3_), channel_id=1, source_target_pairs={{0,63},{1,0},{2,1},{3,2},{4,3},{5,4},{6,5},{7,6},{8,7},{9,8},{10,9... | collective-permute-start | bytes 786440 | tf_op jit(solution)/shard_map/ppermute | solution.py:33
  72.1 4.4 %collective-permute-start.16 = (bf16[16,64,128]{2,1,0:T(8,128)(2,1)S(1)}, bf16[16,64,128]{2,1,0:T(8,128)(2,1)S(1)}, u32[]{:S(2)}, u32[]{:S(2)}) collective-permute-start(bf16[16,64,128]{2,1,0:T(8,128)(2,1)S(1)} %bitcast.26), channel_id=1, source_target_pairs={{0,64},{1,65},{2,66},{3,67},{4,68},{5,69},{6,70},{7,71},{8,72},{9,... | collective-permute-start | bytes 786440 | tf_op jit(solution)/shard_map/ppermute | solution.py:33
